TPU v7x, 256 devices: a whole 4x4x8 slice. The times are simulated.
256 devices in a mesh: gz: 64 (over y, z, core), ma: 4 (over x).
Axes of the slice: x: 4, y: 4, z: 8, core: 2. Of those that a mesh axis runs over, the one named last changes fastest.
Arguments:
- predictor: float32 [3, 64, 512, 512], P(None, 'gz', 'ma'), may hold values from -6 to 6
- stress: float32 [6, 64, 512, 512], P(None, 'gz', 'ma'), may hold values from -6 to 6
- phase: int32 [64, 512, 512], P('gz', 'ma'), may hold values 0 or 1
- old_pressure: float32 [64, 512, 512], P('gz', 'ma'), may hold values from -6 to 6
Outputs:
- velocity: float32 [3, 64, 512, 512], P(None, 'gz', 'ma')
- pressure: float32 [64, 512, 512], P('gz', 'ma')
All inputs are finite; a program needn't handle non-finite values. No bound on the sum of `phase` on one device may be relied on, other than what follows from the above.
Results may differ from a plain program's by a relative error of at most 0.0003.
Values sent between devices are 32-bit elements; how exact they have to be, the bound alone decides.
No kernel may reach another device: no remote copies, remote signals or barrier semaphores. Data moves between devices by JAX's collectives and lax.ppermute only.
A program may use at most 192 MiB of HBM per device.

v0:
```python
import jax
import jax.numpy as jnp
from jax import lax
from jax.sharding import PartitionSpec as P

DENSE_LIQUID = 1.0
DENSE_GAS = 0.1
VISCOUS_LIQUID = 0.5
VISCOUS_GAS = 0.05
TIME_STEP = 0.05
SHIFT_TERM = 0.001
HIGHEST = lax.Precision.HIGHEST


def padded_2(block, sides, width):
    for axis, dim in sides:
        count = lax.axis_size(axis)
        forward = [(i, i + 1) for i in range(count - 1)]
        backward = [(target, source) for source, target in forward]
        low = lax.ppermute(
            lax.slice_in_dim(block, block.shape[dim] - width, None, axis=dim), axis, forward
        )
        high = lax.ppermute(lax.slice_in_dim(block, 0, width, axis=dim), axis, backward)
        block = jnp.concatenate([low, block, high], axis=dim)
    return block


def carried_in(value, axis, join, neutral, backward):
    count, mine = (lax.axis_size(axis), lax.axis_index(axis))
    pieces = jax.tree.map(lambda part: lax.all_gather(part, axis), value)
    if backward:
        pieces = jax.tree.map(lambda part: part[::-1], pieces)
        mine = count - 1 - mine
    running = jax.tree.map(
        lambda part, zero: jnp.full_like(part, 0) + jnp.asarray(zero, part.dtype), value, neutral
    )

    def step(position, running):
        longer = join(running, jax.tree.map(lambda part: part[position], pieces))
        return jax.tree.map(lambda new, old: jnp.where(position < mine, new, old), longer, running)

    return lax.fori_loop(0, count - 1, step, running)


def cosine_table(count):
    index = jnp.arange(count, dtype=jnp.int32)
    product = index[:, None] * (2 * index[None, :] + 1) % (4 * count)
    angle = jnp.pi * product.astype(jnp.float32) / (2.0 * count)
    weight = jnp.where(
        index == 0, jnp.float32((1.0 / count) ** 0.5), jnp.float32((2.0 / count) ** 0.5)
    )
    return weight[:, None] * jnp.cos(angle)


def eigen_part(count, index):
    return 2.0 - 2.0 * jnp.cos(jnp.pi * index.astype(jnp.float32) / count)


def centred(padded, along):
    if along == 0:
        return (padded[..., 1:-1, 2:, 1:-1] - padded[..., 1:-1, :-2, 1:-1]) * 0.5
    if along == 1:
        return (padded[..., 1:-1, 1:-1, 2:] - padded[..., 1:-1, 1:-1, :-2]) * 0.5
    return (padded[..., 2:, 1:-1, 1:-1] - padded[..., :-2, 1:-1, 1:-1]) * 0.5


def laplace(padded):
    centre = padded[..., 1:-1, 1:-1, 1:-1]
    total = padded[..., 1:-1, 2:, 1:-1] + padded[..., 1:-1, :-2, 1:-1]
    total = total + padded[..., 1:-1, 1:-1, 2:] + padded[..., 1:-1, 1:-1, :-2]
    total = total + padded[..., 2:, 1:-1, 1:-1] + padded[..., :-2, 1:-1, 1:-1]
    return total - 6.0 * centre


def predict(padded, predictor, density, viscosity):
    vel_pad = padded[0:3]
    str_pad = padded[3:9]
    old_pad = padded[9]
    lap = laplace(vel_pad)
    force_x = (
        centred(str_pad[0], 0)
        + centred(str_pad[3], 1)
        + centred(str_pad[4], 2)
        + viscosity * lap[0]
    )
    force_y = (
        centred(str_pad[3], 0)
        + centred(str_pad[1], 1)
        + centred(str_pad[5], 2)
        + viscosity * lap[1]
    )
    force_z = (
        centred(str_pad[4], 0)
        + centred(str_pad[5], 1)
        + centred(str_pad[2], 2)
        + viscosity * lap[2]
    )
    force = jnp.stack([force_x, force_y, force_z])
    star = predictor + TIME_STEP / density * force
    old_gradient = jnp.stack([centred(old_pad, 0), centred(old_pad, 1), centred(old_pad, 2)])
    flux = (1.0 - DENSE_GAS / density) * old_gradient
    return (star, flux, old_gradient)


def source_of(padded):
    star_pad = padded[0:3]
    flux_pad = padded[3:6]
    div_star = centred(star_pad[0], 0) + centred(star_pad[1], 1) + centred(star_pad[2], 2)
    div_flux = centred(flux_pad[0], 0) + centred(flux_pad[1], 1) + centred(flux_pad[2], 2)
    return DENSE_GAS / TIME_STEP * div_star + div_flux


def pad_last(field):
    widths = [(0, 0)] * (field.ndim - 1) + [(1, 1)]
    return jnp.pad(field, widths)


def compose(earlier, later):
    return (earlier[0] * later[0], later[0] * earlier[1] + later[1])


def shards(predictor, stress, phase, old_pressure):
    liquid = phase == 1
    density = jnp.where(liquid, jnp.float32(DENSE_LIQUID), jnp.float32(DENSE_GAS))
    viscosity = jnp.where(liquid, jnp.float32(VISCOUS_LIQUID), jnp.float32(VISCOUS_GAS))
    stacked = jnp.concatenate([predictor, stress, old_pressure[None]], 0)
    extended = padded_2(stacked, (("gz", 1), ("ma", 2)), 1)
    star, flux, old_gradient = predict(pad_last(extended), predictor, density, viscosity)
    middle = padded_2(jnp.concatenate([star, flux], 0), (("gz", 1), ("ma", 2)), 1)
    source = source_of(pad_last(middle))
    planes = source.shape[0]
    count_y = source.shape[2]
    count_x = source.shape[1] * lax.axis_size("ma")
    cols_dev = count_y // lax.axis_size("ma")
    table_x = cosine_table(count_x)
    table_y = cosine_table(count_y)
    along_y = jnp.einsum("zxy,ly->zxl", source, table_y, precision=HIGHEST)
    modes = jnp.einsum(
        "kx,zxl->zkl",
        table_x,
        lax.all_to_all(along_y, "ma", split_axis=2, concat_axis=1, tiled=True),
        precision=HIGHEST,
    )
    wave_y = lax.axis_index("ma") * cols_dev + jnp.arange(cols_dev, dtype=jnp.int32)
    spread = (
        SHIFT_TERM
        + eigen_part(count_x, jnp.arange(count_x, dtype=jnp.int32))[:, None]
        + eigen_part(count_y, wave_y)[None, :]
    )
    ratio = 2.0 / (2.0 + spread + jnp.sqrt(spread * (spread + 4.0)))
    zeros = jnp.zeros_like(ratio)
    ones = jnp.ones_like(ratio)
    running = ones
    running = running * ratio
    powers = [running]
    carried = zeros
    plane = 0
    carried = ratio * (carried - modes[plane])
    local_low = carried
    _, entering = carried_in((powers[planes - 1], carried), "gz", compose, (ones, zeros), False)
    lower = [local_low + powers[0] * entering]
    carried = zeros
    local_up = [zeros] * planes
    plane = 0
    carried = ratio * carried + lower[plane]
    local_up[plane] = carried
    _, above = carried_in((powers[planes - 1], carried), "gz", compose, (ones, zeros), True)
    solved = jnp.stack([local_up[0] + powers[planes - 1] * above])
    back_x = jnp.einsum("kx,zkl->zxl", table_x, solved, precision=HIGHEST)
    pressure = jnp.einsum(
        "zxl,ly->zxy",
        lax.all_to_all(back_x, "ma", split_axis=1, concat_axis=2, tiled=True),
        table_y,
        precision=HIGHEST,
    )
    pres_ext = padded_2(pressure, (("gz", 0), ("ma", 1)), 1)
    pres_pad = pad_last(pres_ext)
    gradient = jnp.stack([centred(pres_pad, 0), centred(pres_pad, 1), centred(pres_pad, 2)])
    velocity = star - TIME_STEP * (
        1.0 / DENSE_GAS * gradient + (1.0 / density - 1.0 / DENSE_GAS) * old_gradient
    )
    return (velocity, pressure)


def solution(mesh):
    return jax.shard_map(
        shards,
        mesh=mesh,
        in_specs=(
            P(None, "gz", "ma", None),
            P(None, "gz", "ma", None),
            P("gz", "ma", None),
            P("gz", "ma", None),
        ),
        out_specs=(P(None, "gz", "ma", None), P("gz", "ma", None)),
        check_vma=False,
    )
```

profile of v0, /device:TPU:1, one launch (start us, length us, event | category | flops | bytes accessed | tf_op | source)
XLA Modules:
  0.0 667.3 jit_solution(15293367676409088885)
XLA Ops:
  7.2 2.1 pad_maximum_fusion
  9.3 4.9 collective-permute-start
  14.2 1.9 collective-permute-start.1
  16.2 26.6 %collective-permute-done = f32[10,1,128,512]{3,2,1,0:T(8,128)S(1)} collective-permute-done((f32[10,1,128,512]{3,2,1,0:T(8,128)S(1)}, f32[10,1,128,512]{3,2,1,0:T(8,128)S(1)}, u32[]{:S(2)}, u32[]{:S(2)}) %collective-permute-start) | collective-permute-done | bytes 2621472 | tf_op jit(solution)/shard_map/ppermute | solution.py:20
  42.8 4.4 collective-permute-done.1
  48.2 3.1 collective-permute-start.2
  51.3 1.3 collective-permute-start.3
  52.7 3.6 collective-permute-done.3
  56.3 10.7 %select_maximum_fusion = f32[10,3,130,514]{3,2,1,0:T(8,128)S(1)} fusion(f32[10,3,1,512]{3,2,1,0:T(1,128)S(1)} %collective-permute-done.3, f32[10,3,1,512]{3,2,1,0:T(1,128)S(1)} %collective-permute-done.2, f32[10,1,128,512]{3,2,1,0:T(8,128)S(1)} %collective-permute-done.1, f32[10,1,128,512]{3,2,1,0:T(8,128)S(1)} %collective-permute-done, ...), kind=kLoop, calls=%fused_computation.8 | loop fusion | flops 32073600 | bytes 16005600 | tf_op jit(solution)/shard_map/concatenate | solution.py:24
  67.0 1.5 slice_bitcast_fusion.6
  71.5 3.2 collective-permute-start.4
  74.7 1.9 collective-permute-start.5
  76.6 15.4 %collective-permute-done.4 = f32[6,1,128,512]{3,2,1,0:T(8,128)S(1)} collective-permute-done((f32[6,1,128,512]{3,2,1,0:T(8,128)S(1)}, f32[6,1,128,512]{3,2,1,0:T(8,128)S(1)}, u32[]{:S(2)}, u32[]{:S(2)}) %collective-permute-start.4) | collective-permute-done | bytes 1572896 | tf_op jit(solution)/shard_map/ppermute | solution.py:20
  92.0 4.4 collective-permute-done.5
  96.5 3.1 collective-permute-start.6
  99.6 1.5 collective-permute-start.7
  101.1 3.2 collective-permute-done.7
  104.3 5.3 select_maximum_fusion.6
  110.1 6.0 fusion.23
  116.1 3.4 all-to-all-start
  119.6 5.4 all-to-all-done
  125.1 5.2 bitcast_multiply_fusion.2
  132.3 103.0 %all-gather.5.cloned.1.call-done = f32[64,512,128]{2,1,0:T(8,128)} async-done(((f32[1,512,128]{2,1,0:T(8,128)}), f32[64,512,128]{2,1,0:T(8,128)}) %all-gather.5.cloned.1.call-update) | async-done | bytes 16777232 | tf_op jit(solution)/shard_map/all_gather | solution.py:30
  235.4 100.3 %all-gather.7.cloned.1.call-done = f32[64,512,128]{2,1,0:T(8,128)} async-done(((f32[1,512,128]{2,1,0:T(8,128)}), f32[64,512,128]{2,1,0:T(8,128)}) %all-gather.7.cloned.1.call-update) | async-done | bytes 16777232 | tf_op jit(solution)/shard_map/all_gather | solution.py:30
  335.7 80.0 %while.28 = (s32[]{:T(128)}, f32[512,128]{1,0:T(8,128)S(1)}, s32[]{:T(128)}, f32[64,512,128]{2,1,0:T(8,128)}, f32[64,512,128]{2,1,0:T(8,128)}, /*index=5*/s32[]{:T(128)}, s32[]{:T(128)}) while((s32[]{:T(128)}, f32[512,128]{1,0:T(8,128)S(1)}, s32[]{:T(128)}, f32[64,512,128]{2,1,0:T(8,128)}, f32[64,512,128]{2,1,0:T(8,128)}, ...), condition=%wide.region_1.2_spmd.clone, body=%wide.region_0.1_spmd.clone.sunk | while | flops 262148 | bytes 1048677 | solution.py:42
  339.5 1.2 fusion.108
  343.3 1.2 fusion.108
  347.1 1.2 fusion.108
  350.9 1.2 fusion.108
  354.7 1.2 fusion.108
  356.0 1.2 fusion.108
  359.8 1.2 fusion.108
  363.6 1.2 fusion.108
  367.4 1.2 fusion.108
  416.8 11.6 %rev.6 = f32[64,512,128]{2,1,0:T(8,128)} reverse(f32[64,512,128]{2,1,0:T(8,128)} %get-tuple-element.416), dimensions={0} | reverse | bytes 33554432 | tf_op jit(solution)/shard_map/rev | solution.py:32
  428.4 85.4 %all-gather.9.cloned.1.call-done = f32[32768,128]{0,1:T(8,128)} async-done(((f32[512,128]{0,1:T(8,128)}), f32[32768,128]{0,1:T(8,128)}) %all-gather.9.cloned.1.call-update) | async-done | bytes 16777232 | tf_op jit(solution)/shard_map/all_gather | solution.py:30
  513.8 17.4 %copy.36 = f32[32768,128]{1,0:T(8,128)} copy(f32[32768,128]{0,1:T(8,128)} %all-gather.9.cloned.1.call-done) | data formatting | bytes 33554432 | tf_op jit(solution)/shard_map/all_gather | solution.py:30
  531.2 11.5 %rev.7 = f32[64,512,128]{2,1,0:T(8,128)} reverse(f32[64,512,128]{2,1,0:T(8,128)} %bitcast.118), dimensions={0} | reverse | bytes 33554432 | tf_op jit(solution)/shard_map/rev | solution.py:32
  542.7 80.1 %while.29 = (s32[]{:T(128)}, f32[512,128]{1,0:T(8,128)S(1)}, s32[]{:T(128)}, f32[64,512,128]{2,1,0:T(8,128)}, f32[64,512,128]{2,1,0:T(8,128)}, /*index=5*/s32[]{:T(128)}, s32[]{:T(128)}) while((s32[]{:T(128)}, f32[512,128]{1,0:T(8,128)S(1)}, s32[]{:T(128)}, f32[64,512,128]{2,1,0:T(8,128)}, f32[64,512,128]{2,1,0:T(8,128)}, ...), condition=%wide.region_3.4_spmd.clone, body=%wide.region_2.3_spmd.clone.sunk | while | flops 262148 | bytes 1048677 | solution.py:42
  622.9 4.7 convolution_bitcast_fusion.1
  627.8 10.0 %all_to_all.30 = f32[1,512,128]{2,0,1:T(1,128)S(1)} all-to-all(f32[1,512,128]{2,0,1:T(1,128)S(1)} %copy.34), channel_id=1, replica_groups=mesh['gz'=64,'ma'=4] {'ma'}, dimensions={1} | all-to-all | bytes 524288 | tf_op jit(solution)/shard_map/all_to_all | solution.py:172
  637.9 4.6 convolution_bitcast_fusion
  642.6 2.6 collective-permute-start.8
  645.2 2.0 collective-permute-start.9
  647.2 1.3 collective-permute-done.8
  648.5 4.4 collective-permute-done.9
  652.9 1.3 collective-permute-start.10
  654.2 4.0 collective-permute-start.11
  (169 shorter events, 156.9 us)
Async XLA Ops:
  7.2 40.0 %copy-start = (f32[6,1,128,512]{3,2,1,0:T(8,128)S(1)}, f32[6,1,128,512]{3,2,1,0:T(8,128)}, u32[]{:S(2)}) copy-start(f32[6,1,128,512]{3,2,1,0:T(8,128)} %param.9) | copy-start | bytes 4718596
  7.2 45.4 %copy-start.6 = (s32[1,128,512]{2,1,0:T(8,128)S(1)}, s32[1,128,512]{2,1,0:T(8,128)}, u32[]{:S(2)}) copy-start(s32[1,128,512]{2,1,0:T(8,128)} %param.10) | copy-start | bytes 786436
  7.2 49.1 %copy-start.1 = (f32[3,1,128,512]{3,2,1,0:T(8,128)S(1)}, f32[3,1,128,512]{3,2,1,0:T(8,128)}, u32[]{:S(2)}) copy-start(f32[3,1,128,512]{3,2,1,0:T(8,128)} %param.8) | copy-start | bytes 2359300
  7.2 49.1 %copy-start.2 = (f32[1,128,512]{2,1,0:T(8,128)S(1)}, f32[1,128,512]{2,1,0:T(8,128)}, u32[]{:S(2)}) copy-start(f32[1,128,512]{2,1,0:T(8,128)} %param.11) | copy-start | bytes 786436
  9.3 33.5 %collective-permute-start = (f32[10,1,128,512]{3,2,1,0:T(8,128)S(1)}, f32[10,1,128,512]{3,2,1,0:T(8,128)S(1)}, u32[]{:S(2)}, u32[]{:S(2)}) collective-permute-start(f32[10,1,128,512]{3,2,1,0:T(8,128)S(1)} %pad_maximum_fusion), channel_id=1, source_target_pairs={{0,4},{4,8},{8,12},{12,16},{16,20},{20,24},{24,28},{28,32},{32,36}... | collective-permute-start | bytes 7864328 | tf_op jit(solution)/shard_map/ppermute | solution.py:20
  14.2 33.0 %collective-permute-start.1 = (f32[10,1,128,512]{3,2,1,0:T(8,128)S(1)}, f32[10,1,128,512]{3,2,1,0:T(8,128)S(1)}, u32[]{:S(2)}, u32[]{:S(2)}) collective-permute-start(f32[10,1,128,512]{3,2,1,0:T(8,128)S(1)} %pad_maximum_fusion), channel_id=1, source_target_pairs={{4,0},{8,4},{12,8},{16,12},{20,16},{24,20},{28,24},{32,28},{36,32}... | collective-permute-start | bytes 7864328 | tf_op jit(solution)/shard_map/ppermute | solution.py:23
  48.2 4.5 collective-permute-start.2
  51.3 5.0 collective-permute-start.3
  68.9 1.2 copy-start.4
  71.5 20.5 %collective-permute-start.4 = (f32[6,1,128,512]{3,2,1,0:T(8,128)S(1)}, f32[6,1,128,512]{3,2,1,0:T(8,128)S(1)}, u32[]{:S(2)}, u32[]{:S(2)}) collective-permute-start(f32[6,1,128,512]{3,2,1,0:T(8,128)S(1)} %pad_maximum_fusion.1), channel_id=1, source_target_pairs={{0,4},{4,8},{8,12},{12,16},{16,20},{20,24},{24,28},{28,32},{32,36}... | collective-permute-start | bytes 4718600 | tf_op jit(solution)/shard_map/ppermute | solution.py:20
  74.7 21.7 %collective-permute-start.5 = (f32[6,1,128,512]{3,2,1,0:T(8,128)S(1)}, f32[6,1,128,512]{3,2,1,0:T(8,128)S(1)}, u32[]{:S(2)}, u32[]{:S(2)}) collective-permute-start(f32[6,1,128,512]{3,2,1,0:T(8,128)S(1)} %pad_maximum_fusion.1), channel_id=1, source_target_pairs={{4,0},{8,4},{12,8},{16,12},{20,16},{24,20},{28,24},{32,28},{36,32}... | collective-permute-start | bytes 4718600 | tf_op jit(solution)/shard_map/ppermute | solution.py:23
  96.5 4.6 collective-permute-start.6
  99.6 4.7 collective-permute-start.7
  116.1 8.9 %all-to-all-start = ((f32[1,128,512]{1,0,2:T(1,128)}), f32[1,128,512]{1,0,2:T(1,128)S(1)}, u32[]{:S(2)}, u32[]{:S(2)}) async-start(f32[1,128,512]{1,0,2:T(1,128)} %bitcast.53), calls=%async_computation | async-start | bytes 524288 | tf_op jit(solution)/shard_map/all_to_all | solution.py:141
  119.5 115.9 %all-gather.5.cloned.1.call-start = ((), (), s32[]{:S(2)}) async-start(), calls=%async_computation.2 | async-start | bytes 17039360 | tf_op jit(solution)/shard_map/all_gather | solution.py:30
  131.1 204.5 %all-gather.7.cloned.1.call-start = ((), (), s32[]{:S(2)}) async-start(), calls=%async_computation.3 | async-start | bytes 17039360 | tf_op jit(solution)/shard_map/all_gather | solution.py:30
  132.0 381.7 %all-gather.9.cloned.1.call-start = ((), (), s32[]{:S(2)}) async-start(), calls=%async_computation.4 | async-start | bytes 17039360 | tf_op jit(solution)/shard_map/all_gather | solution.py:30
  531.2 91.7 %copy-start.5 = (f32[512,128]{0,1:T(8,128)S(1)}, f32[512,128]{0,1:T(8,128)}, u32[]{:S(2)}) copy-start(f32[512,128]{0,1:T(8,128)} %fusion.79) | copy-start | bytes 786436
  642.6 18.2 %copy-start.3 = (f32[1,128,512]{2,1,0:T(8,128)}, f32[1,128,512]{2,1,0:T(8,128)S(1)}, u32[]{:S(2)}) copy-start(f32[1,128,512]{2,1,0:T(8,128)S(1)} %convolution_bitcast_fusion) | copy-start | bytes 786436
  642.6 5.9 collective-permute-start.8
  645.2 7.7 %collective-permute-start.9 = (f32[1,128,512]{2,1,0:T(8,128)S(1)}, f32[1,128,512]{2,1,0:T(8,128)S(1)}, u32[]{:S(2)}, u32[]{:S(2)}) collective-permute-start(f32[1,128,512]{2,1,0:T(8,128)S(1)} %convolution_bitcast_fusion), channel_id=1, source_target_pairs={{4,0},{8,4},{12,8},{16,12},{20,16},{24,20},{28,24},{32,28},{36,32}... | collective-permute-start | bytes 786440 | tf_op jit(solution)/shard_map/ppermute | solution.py:23
  652.9 5.3 collective-permute-start.10
  654.2 4.8 collective-permute-start.11
Sparse Core Ops, SparseCore 0:
  131.3 104.0 all-gather.4
  238.7 96.8 all-gather.6
  416.9 96.8 all-gather.8
where the time goes:
time: 672 us; the launch traced here: 667 us
  waiting for transfers between devices  358 us (53%)
  other arithmetic  182 us (27%)
  local copies, waits for them, and re-layouts  45 us (7%)
  starting transfers between devices  34.6 us (5%)
  matrix products  20.5 us (3%)
  between operations  14.1 us (2%)
  blocking collectives  10 us (1%)
    all_gather x3, waiting for transfers between devices, carried_in(): pieces = jax.tree.map(lambda part: lax.all_gather(part, axis), value)  289 us
    select_n x126, other arithmetic, step(): jnp.where(position < mine, new, old)  157 us
    ppermute x6, waiting for transfers between devices, padded_2(): lax.ppermute(lax.slice_in_dim(block, block.shape[dim] - width, None, axis...  44.1 us
    rev x2, local copies, waits for them, and re-layouts, carried_in(): pieces = jax.tree.map(lambda part: part[::-1], pieces)  23.1 us
    ppermute x6, starting transfers between devices, padded_2(): lax.ppermute(lax.slice_in_dim(block, block.shape[dim] - width, None, axis...  21 us
    ppermute x6, waiting for transfers between devices, padded_2(): lax.ppermute(lax.slice_in_dim(block, 0, width, axis=dim), axis, backward)  20 us
    all_gather x1, local copies, waits for them, and re-layouts, carried_in(): pieces = jax.tree.map(lambda part: lax.all_gather(part, axis), value)  17.4 us
    concatenate x4, other arithmetic, padded_2(): block = jnp.concatenate([low, block, high], axis=dim)  16.4 us
  transfers between devices with their start and end apart: 16, of which 13 were waited for; matrix products, arithmetic and copies ran while one was open for 2% of the time, Pallas kernels for 0%

commit v1 on v0

v1 whole, which is shorter than its diff:
```python
import jax
import jax.numpy as jnp
import numpy as np
from jax import lax
from jax.experimental import pallas as pl
from jax.experimental.pallas import tpu as pltpu
from jax.sharding import PartitionSpec as P

SHIFT_TERM = 0.001
VISCOUS = 0.025
STRESS_LIQUID = 0.025
STRESS_GAS = 0.25
OLD_LIQUID = 0.225
VMEM_LIMIT = 16 * 1024 * 1024
F32 = jnp.float32
BF16 = jnp.bfloat16


def cosine_parts(count):
    index = np.arange(count, dtype=np.int64)
    product = index[:, None] * (2 * index[None, :] + 1) % (4 * count)
    angle = np.pi * product.astype(np.float64) / (2.0 * count)
    weight = np.where(index == 0, (1.0 / count) ** 0.5, (2.0 / count) ** 0.5)
    table = (weight[:, None] * np.cos(angle)).astype(np.float32)
    high = table.astype(BF16)
    low = (table - high.astype(np.float32)).astype(BF16)
    return high, low


def eigen_parts(count):
    index = np.arange(count).astype(np.float32)
    angle = np.float32(np.pi) * index / np.float32(count)
    return np.float32(2.0) - np.float32(2.0) * np.cos(angle).astype(np.float32)


def split(value):
    high = value.astype(BF16)
    return high, (value - high.astype(F32)).astype(BF16)


def product_3(a, b, dims):
    def dot(x, y):
        return lax.dot_general(x, y, (dims, ((), ())), preferred_element_type=F32)

    return dot(a[0], b[0]) + (dot(a[0], b[1]) + dot(a[1], b[0]))


def whole():
    return pl.BlockSpec(memory_space=pltpu.VMEM)


def call(body, outs, args, flops, scratch=()):
    shapes = [jax.ShapeDtypeStruct(shape, F32) for shape in outs]
    moved = sum(a.size * a.dtype.itemsize for a in args) + sum(4 * s.size for s in shapes)
    return pl.pallas_call(
        body,
        out_shape=shapes,
        in_specs=[whole() for _ in args],
        out_specs=[whole() for _ in outs],
        scratch_shapes=list(scratch),
        cost_estimate=pl.CostEstimate(flops=flops, bytes_accessed=moved, transcendentals=0),
        compiler_params=pltpu.CompilerParams(vmem_limit_bytes=VMEM_LIMIT),
    )(*args)


def rows_body(pred, stress, old, even_row, odd_row):
    rows = old.shape[1]
    even = lax.axis_index("ma") % 2 == 0

    planes = [pred.at[i, 0] for i in range(3)] + [stress.at[i, 0] for i in (0, 3, 4)] + [old.at[0]]
    for i, plane in enumerate(planes):
        low, high = plane[0:1], plane[rows - 1 : rows]
        even_row[i : i + 1] = jnp.where(even, high, low)
        odd_row[i : i + 1] = jnp.where(even, low, high)
    even_row[7:8] = jnp.zeros_like(even_row[7:8])
    odd_row[7:8] = jnp.zeros_like(odd_row[7:8])


def send_body(pred, stress, old, far_phase, near_phase, _, far, near):
    odd = lax.axis_index("gz") % 2 == 1
    far_sign = jnp.where(odd, F32(-1), F32(1))
    for out, phase, sign in ((far, far_phase, far_sign), (near, near_phase, -far_sign)):
        liquid = phase[0] == 1
        half = jnp.where(liquid, sign * STRESS_LIQUID, sign * STRESS_GAS)
        out[0] = VISCOUS * pred[0, 0] + half * stress[4, 0]
        out[1] = VISCOUS * pred[1, 0] + half * stress[5, 0]
        push = jnp.where(liquid, sign * OLD_LIQUID, 0.0)
        out[2] = VISCOUS * pred[2, 0] + half * stress[2, 0] + push * old[0]


def shifted(value, low_row=None, high_row=None):
    rows = value.shape[0]
    spot = lax.broadcasted_iota(jnp.int32, value.shape, 0)
    low_row = F32(0) if low_row is None else low_row
    high_row = F32(0) if high_row is None else high_row
    below = jnp.where(spot == 0, low_row, pltpu.roll(value, 1, 0))
    above = jnp.where(spot == rows - 1, high_row, pltpu.roll(value, rows - 1, 0))
    return below, above


def shifted_y(value):
    columns = value.shape[1]
    spot = lax.broadcasted_iota(jnp.int32, value.shape, 1)
    below = jnp.where(spot == 0, 0.0, pltpu.roll(value, 1, 1))
    above = jnp.where(spot == columns - 1, 0.0, pltpu.roll(value, columns - 1, 1))
    return below, above


def local_body(pred, stress, phase, old, even_row, odd_row, out):
    even = lax.axis_index("ma") % 2 == 0
    before = jnp.where(even, odd_row[...], even_row[...])
    after = jnp.where(even, even_row[...], odd_row[...])
    liquid = phase[0] == 1
    half = jnp.where(liquid, STRESS_LIQUID, STRESS_GAS)

    def along_x(value, row):
        below, above = shifted(value, before[row : row + 1], after[row : row + 1])
        return above - below

    def along_y(value):
        below, above = shifted_y(value)
        return above - below

    for i in range(3):
        centre = pred[i, 0]
        below, above = shifted(centre, before[i : i + 1], after[i : i + 1])
        left, right = shifted_y(centre)
        total = centre + VISCOUS * ((below + above) + (left + right) - 6.0 * centre)
        if i == 0:
            force = along_x(stress[0, 0], 3) + along_y(stress[3, 0])
            push = along_x(old[0], 6)
        elif i == 1:
            force = along_x(stress[3, 0], 4) + along_y(stress[1, 0])
            push = along_y(old[0])
        else:
            force = along_x(stress[4, 0], 5) + along_y(stress[5, 0])
            push = None
        total = total + half * force
        if push is not None:
            total = total + jnp.where(liquid, OLD_LIQUID * push, 0.0)
        out[i] = total


def source_body(local, far, near, high, low, out, sent):
    u_x = local[0] + (far[0] + near[0])
    u_y = local[1] + (far[1] + near[1])
    u_z = local[2] + (far[2] + near[2])
    out[0], out[1], out[2] = u_x, u_y, u_z
    behind, ahead = shifted(u_x)
    left, right = shifted_y(u_y)
    planar = (ahead - behind) + (right - left)
    table = (high[...], low[...])
    nt = ((1,), (1,))
    pairs = sent.shape[0] // 5
    for i, value in enumerate((planar, u_z)):
        modes = product_3(table, split(value), nt)
        sent[pl.ds(2 * i, pairs, 5)] = modes[:pairs]
        sent[pl.ds(2 * i + 1, pairs, 5)] = modes[pairs:]
    rows, columns = u_x.shape
    first, last = u_x[0:1], u_x[rows - 1 : rows]
    spot = lax.broadcasted_iota(jnp.int32, (128, columns), 0)
    zero = jnp.zeros((128, columns), F32)
    lead = jnp.where(spot == 0, first, jnp.where(spot == 1, last, zero))
    trail = jnp.where(spot == 2, first, jnp.where(spot == 3, last, zero))
    ends = product_3((high[:pairs], low[:pairs]), split(lead), nt)
    ends = ends + product_3((high[pairs:], low[pairs:]), split(trail), nt)
    sent[pl.ds(4, pairs, 5)] = ends


def solve_body(blocks, received, ratio, high, low, sent, held, result):
    planes = received.shape[0] // (5 * blocks)
    step = 5 * blocks
    tiles = ratio.shape[0] // 2
    lane = lax.broadcasted_iota(jnp.int32, (planes, 128), 1)
    row = lax.broadcasted_iota(jnp.int32, (planes, 128), 0)
    ends = [received[pl.ds(5 * b + 4, planes, step)] for b in range(blocks)]
    sides = []
    for j in range(2):
        parts = []
        for b in range(blocks):
            source = received[pl.ds(5 * b + j, planes, step)]
            if b + 1 < blocks:
                source = source + jnp.where(lane == 127, ends[b + 1][:, 2 * j : 2 * j + 1], 0.0)
            if b > 0:
                source = source - jnp.where(lane == 0, ends[b - 1][:, 2 * j + 1 : 2 * j + 2], 0.0)
            u_z = received[pl.ds(5 * b + 2 + j, planes, step)]
            up = jnp.where(row == planes - 1, 0.0, pltpu.roll(u_z, planes - 1, 0))
            down = jnp.where(row == 0, 0.0, pltpu.roll(u_z, 1, 0))
            parts.append(source + (up - down))
        sides.append(jnp.concatenate(parts, 1))
    table = (high[...], low[...])
    modes = product_3(split(jnp.concatenate(sides, 0)), table, ((1,), (1,)))
    every = 2 * tiles
    for j in range(2):
        for t in range(tiles):
            held[pl.ds(j * tiles + t, planes, every)] = modes[
                j * planes : (j + 1) * planes, t * 128 : (t + 1) * 128
            ]
    r = ratio[...]
    carry = jnp.zeros_like(r)
    for z in range(planes):
        carry = r * (carry - held[every * z : every * (z + 1)])
        held[every * z : every * (z + 1)] = carry
    carry = jnp.zeros_like(r)
    result[0:every] = carry
    result[every * (planes + 1) : every * (planes + 2)] = carry
    for z in reversed(range(planes)):
        carry = r * carry + held[every * z : every * (z + 1)]
        result[every * (z + 1) : every * (z + 2)] = carry
    fields = []
    for j in range(2):
        pieces = [result[pl.ds(every + j * tiles + t, planes, every)] for t in range(tiles)]
        fields.append(jnp.concatenate(pieces, 1))
    for j in range(2):
        pieces = [
            result[pl.ds(2 * every + j * tiles + t, planes, every)]
            - result[pl.ds(j * tiles + t, planes, every)]
            for t in range(tiles)
        ]
        fields.append(jnp.concatenate(pieces, 1))
    back = product_3(split(jnp.concatenate(fields, 0)), table, ((1,), (0,)))
    for i in range(4):
        for b in range(blocks):
            sent[pl.ds(5 * b + i, planes, step)] = back[
                i * planes : (i + 1) * planes, b * 128 : (b + 1) * 128
            ]
    for b in range(blocks):
        edge = jnp.zeros((planes, 128), F32)
        for j in range(2):
            mine = back[j * planes : (j + 1) * planes]
            if b > 0:
                edge = jnp.where(lane == 2 * j, mine[:, b * 128 - 1 : b * 128], edge)
            if b + 1 < blocks:
                edge = jnp.where(
                    lane == 2 * j + 1, mine[:, b * 128 + 128 : b * 128 + 129], edge
                )
        sent[pl.ds(5 * b + 4, planes, step)] = edge


def final_body(received, u, high, low, velocity, pressure):
    pairs = received.shape[0] // 5
    table = (high[...], low[...])
    nn = ((1,), (0,))

    def field(i):
        pieces = [received[pl.ds(i + j, pairs, 5)] for j in range(2)]
        return product_3(split(jnp.concatenate(pieces, 0).T), table, nn)

    p = field(0)
    along_z = field(2)
    ends = split(received[pl.ds(4, pairs, 5)].T[0:8])
    lead = product_3(ends, (high[:pairs], low[:pairs]), nn)
    trail = product_3(ends, (high[pairs:], low[pairs:]), nn)
    behind, ahead = shifted(p, lead[0:1] + trail[2:3], lead[1:2] + trail[3:4])
    left, right = shifted_y(p)
    pressure[0] = p
    velocity[0, 0] = u[0] - 0.25 * (ahead - behind)
    velocity[1, 0] = u[1] - 0.25 * (right - left)
    velocity[2, 0] = u[2] - 0.25 * along_z


def shards(predictor, stress, phase, old_pressure):
    planes_z, lines = lax.axis_size("gz"), lax.axis_size("ma")
    rows, columns = old_pressure.shape[1], old_pressure.shape[2]
    devices = planes_z * lines
    table = cosine_parts(columns)
    high, low = jnp.asarray(table[0]), jnp.asarray(table[1])
    eigen = eigen_parts(columns)

    def swap(value, axis, begin):
        pairs = [(i, i + 1) for i in range(begin, lax.axis_size(axis) - 1, 2)]
        return lax.ppermute(value, axis, pairs + [(b, a) for a, b in pairs])

    far_phase = swap(phase, "gz", 1)
    near_phase = swap(phase, "gz", 0)
    even_row, odd_row = call(
        rows_body, [(8, columns), (8, columns)], (predictor, stress, old_pressure), 10000
    )
    far, near = call(
        send_body,
        [(3, rows, columns), (3, rows, columns)],
        (predictor, stress, old_pressure, far_phase, near_phase, even_row),
        1000000,
    )
    even_row = swap(even_row, "ma", 0)
    odd_row = swap(odd_row, "ma", 1)
    far = swap(far, "gz", 1)
    near = swap(near, "gz", 0)

    own = lax.axis_index("gz") * lines + lax.axis_index("ma")
    tiles = columns // 128
    part_x = jnp.asarray(np.tile(eigen.reshape(tiles, 128), (2, 1)))
    pair = lax.dynamic_index_in_dim(
        jnp.asarray(eigen.reshape(2, devices)), own, 1, keepdims=False
    )
    part_y = jnp.repeat(pair, tiles)[:, None]
    spread = SHIFT_TERM + part_x + part_y
    ratio = 2.0 / (2.0 + spread + jnp.sqrt(spread * (spread + 4.0)))

    (local,) = call(
        local_body,
        [(3, rows, columns)],
        (predictor, stress, phase, old_pressure, even_row, odd_row),
        8000000,
    )
    u, modes = call(
        source_body,
        [(3, rows, columns), (5 * devices, 128)],
        (local, far, near, high, low),
        600000000,
    )

    def exchange(value):
        moved = lax.all_to_all(value.reshape(5 * devices, 1, 128), ("gz", "ma"), 0, 0, tiled=True)
        return moved.reshape(5 * devices, 128)

    (solved,) = call(
        lambda *refs: solve_body(lines, *refs),
        [(5 * devices, 128)],
        (exchange(modes), ratio, high, low),
        700000000,
        (
            pltpu.VMEM((2 * tiles * planes_z, 128), F32),
            pltpu.VMEM((2 * tiles * (planes_z + 2), 128), F32),
        ),
    )
    velocity, pressure = call(
        final_body,
        [(3, 1, rows, columns), (1, rows, columns)],
        (exchange(solved), u, high, low),
        500000000,
    )
    return velocity, pressure


def solution(mesh):
    return jax.shard_map(
        shards,
        mesh=mesh,
        in_specs=(
            P(None, "gz", "ma", None),
            P(None, "gz", "ma", None),
            P("gz", "ma", None),
            P("gz", "ma", None),
        ),
        out_specs=(P(None, "gz", "ma", None), P("gz", "ma", None)),
        check_vma=False,
    )
```

time: 672 us -> 100 us (0.15)
  waiting for transfers between devices: 358 us -> 30 us
  other arithmetic: 182 us -> 0.08 us
  local copies, waits for them, and re-layouts: 45 us -> 4.36 us
  matrix products: 20.5 us -> 0 us
  blocking collectives: 10 us -> 29.7 us
  between operations: 14.1 us -> 0.74 us
  Pallas kernels: 0 us -> 7.25 us
  starting transfers between devices: 34.6 us -> 27.6 us
    all_gather x3 -> x0, waiting for transfers between devices: 289 us -> none  [carried_in(): pieces = jax.tree.map(lambda part: lax.all_gather(part, axis), value)]
    select_n x126 -> x0, other arithmetic: 157 us -> none  [step(): jnp.where(position < mine, new, old)]
    ppermute x12 -> x6, waiting for transfers between devices: 64 us -> 6.89 us  [swap(): return lax.ppermute(value, axis, pairs + [(b, a) for a, b in pairs])]
    rev x2 -> x0, local copies, waits for them, and re-layouts: 23.1 us -> none  [carried_in(): pieces = jax.tree.map(lambda part: part[::-1], pieces)]
    dot_general x4 -> x0, matrix products: 20.5 us -> none  [the longest x1 5.99 us: shards(): along_y = jnp.einsum('zxy,ly->zxl', source, table_y, precision=HIGHEST)]
    ppermute x12 -> x6, starting transfers between devices: 30.8 us -> 10.8 us  [swap(): return lax.ppermute(value, axis, pairs + [(b, a) for a, b in pairs])]
    all_to_all x1, blocking collectives: 10 us -> 29.7 us  [exchange(): lax.all_to_all(value.reshape(5 * devices, 1, 128), ('gz', 'ma'), 0, 0, ti...]
    concatenate x6 -> x0, other arithmetic: 18.7 us -> none  [the longest x4 16.4 us: padded_2(): block = jnp.concatenate([low, block, high], axis=dim)]
  transfers between devices with their start and end apart: 16 -> 7, of which waited for: 13 -> 4; matrix products, arithmetic and copies ran while one was open for 2% -> 1% of each run, Pallas kernels for 0% -> 1%
where the time goes in v1:
time: 100 us; the launch traced here: 99.7 us
  waiting for transfers between devices  30 us (30%)
  blocking collectives  29.7 us (30%)
  starting transfers between devices  27.6 us (28%)
  Pallas kernels  7.25 us (7%)
  local copies, waits for them, and re-layouts  4.36 us (4%)
    all_to_all x1, blocking collectives, exchange(): lax.all_to_all(value.reshape(5 * devices, 1, 128), ('gz', 'ma'), 0, 0, ti...  29.7 us
    all_to_all x1, waiting for transfers between devices, exchange(): lax.all_to_all(value.reshape(5 * devices, 1, 128), ('gz', 'ma'), 0, 0, ti...  23.1 us
    all_to_all x1, starting transfers between devices, exchange(): lax.all_to_all(value.reshape(5 * devices, 1, 128), ('gz', 'ma'), 0, 0, ti...  16.8 us
    ppermute x6, starting transfers between devices, swap(): return lax.ppermute(value, axis, pairs + [(b, a) for a, b in pairs])  10.8 us
    pallas_call x6, Pallas kernels, call(): pl.pallas_call(body, out_shape=shapes, in_specs=[whole() for _ in args],...  7.25 us
    ppermute x6, waiting for transfers between devices, swap(): return lax.ppermute(value, axis, pairs + [(b, a) for a, b in pairs])  6.89 us
    unnamed x14, local copies, waits for them, and re-layouts  3.5 us
  transfers between devices with their start and end apart: 7, of which 4 were waited for; matrix products, arithmetic and copies ran while one was open for 1% of the time, Pallas kernels for 1%

profile of v1, /device:TPU:1, one launch (start us, length us, event | category | flops | bytes accessed | tf_op | source)
XLA Modules:
  0.0 99.7 jit_solution(8652565332803611259)
XLA Ops:
  0.6 4.9 %collective-permute-start.2 = (s32[1,128,512]{2,1,0:T(8,128)}, s32[1,128,512]{2,1,0:T(8,128)S(1)}, u32[]{:S(2)}, u32[]{:S(2)}) collective-permute-start(s32[1,128,512]{2,1,0:T(8,128)} %phase.1), channel_id=1, source_target_pairs={{4,8},{12,16},{20,24},{28,32},{36,40},{44,48},{52,56},{60,64},{68,... | collective-permute-start | bytes 786440 | tf_op jit(solution)/shard_map/ppermute | solution.py:272
  5.6 0.1 collective-permute-start.3
  5.7 0.0 copy-start
  5.7 1.4 %copy-done = f32[6,1,128,512]{3,2,1,0:T(8,128)S(1)} copy-done((f32[6,1,128,512]{3,2,1,0:T(8,128)S(1)}, f32[6,1,128,512]{3,2,1,0:T(8,128)}, u32[]{:S(2)}) %copy-start) | copy-done | bytes 1572888
  7.1 0.0 copy-start.1
  7.1 1.1 %copy-done.1 = f32[3,1,128,512]{3,2,1,0:T(8,128)S(1)} copy-done((f32[3,1,128,512]{3,2,1,0:T(8,128)S(1)}, f32[3,1,128,512]{3,2,1,0:T(8,128)}, u32[]{:S(2)}) %copy-start.1) | copy-done | bytes 786456
  8.2 0.0 copy-start.2
  8.2 0.9 copy-done.2
  9.2 0.6 collective-permute-done.2.far_phase
  9.8 0.0 collective-permute-done.3.near_phase
  9.8 0.0 copy-start.5
  9.8 0.3 shard_map.97
  10.1 3.6 %collective-permute-start.4 = (f32[3,128,512]{2,1,0:T(8,128)S(1)}, f32[3,128,512]{2,1,0:T(8,128)S(1)}, u32[]{:S(2)}, u32[]{:S(2)}) collective-permute-start(f32[3,128,512]{2,1,0:T(8,128)S(1)} %get-tuple-element.10), channel_id=1, source_target_pairs={{4,8},{12,16},{20,24},{28,32},{36,40},{44,48},{52,56},{60,64},{68,... | collective-permute-start | bytes 2359304 | tf_op jit(solution)/shard_map/ppermute | solution.py:272
  13.8 0.1 collective-permute-start.5
  13.9 1.3 %collective-permute-start = (f32[8,512]{1,0:T(8,128)S(1)}, f32[8,512]{1,0:T(8,128)S(1)}, u32[]{:S(2)}, u32[]{:S(2)}) collective-permute-start(f32[8,512]{1,0:T(8,128)S(1)} %get-tuple-element.8._), channel_id=1, source_target_pairs={{0,1},{2,3},{1,0},{3,2},{4,5},{6,7},{5,4},{7,6},{8,9},{10,11},{9,8... | collective-permute-start | bytes 49160 | tf_op jit(solution)/shard_map/ppermute | solution.py:272
  15.2 0.0 copy-start.3
  15.2 0.0 copy-start.4
  15.2 0.8 collective-permute-start.1
  16.0 0.6 collective-permute-done.even_row
  16.6 0.0 collective-permute-done.1.odd_row
  16.6 0.0 copy-done.5
  16.6 1.2 %shard_map.96.local = f32[3,128,512]{2,1,0:T(8,128)S(1)} custom-call(f32[3,1,128,512]{3,2,1,0:T(8,128)S(1)} %copy-done.1, f32[6,1,128,512]{3,2,1,0:T(8,128)S(1)} %copy-done, s32[1,128,512]{2,1,0:T(8,128)S(1)} %copy-done.5, f32[1,128,512]{2,1,0:T(8,128)S(1)} %copy-done.2, f32[8,512]{1,0:T(8,128)S(1)} %collective-permute-done.even_row, ...), custom_call_target="tpu_custom_call" | custom-call | flops 8000000 | bytes 3702784 | tf_op jit(solution)/shard_map/pallas_call | solution.py:55
  17.8 0.0 copy-start.6
  17.8 5.7 %collective-permute-done.4.far = f32[3,128,512]{2,1,0:T(8,128)S(1)} collective-permute-done((f32[3,128,512]{2,1,0:T(8,128)S(1)}, f32[3,128,512]{2,1,0:T(8,128)S(1)}, u32[]{:S(2)}, u32[]{:S(2)}) %collective-permute-start.4) | collective-permute-done | bytes 786464 | tf_op jit(solution)/shard_map/ppermute | solution.py:272
  23.4 0.0 collective-permute-done.5.near
  23.4 0.0 copy-done.3
  23.4 0.0 copy-done.4
  23.4 2.4 %shard_map.98 = (f32[3,128,512]{2,1,0:T(8,128)S(1)}, f32[1280,128]{1,0:T(8,128)}) custom-call(f32[3,128,512]{2,1,0:T(8,128)S(1)} %shard_map.96.local, f32[3,128,512]{2,1,0:T(8,128)S(1)} %collective-permute-done.4.far, f32[3,128,512]{2,1,0:T(8,128)S(1)} %collective-permute-done.5.near, bf16[512,512]{1,0:T(8,128)(2,1)S(1)} %copy-done.3, ...), custom_call_target="tpu_custom_call" | custom-call | flops 600000000 | bytes 4849664 | tf_op jit(solution)/shard_map/pallas_call | solution.py:55
  25.9 16.8 %all-to-all-start = ((f32[1280,1,128]{2,1,0:T(1,128)}), f32[1280,1,128]{2,1,0:T(1,128)S(1)}, u32[]{:S(2)}, u32[]{:S(2)}) async-start(f32[1280,1,128]{2,1,0:T(1,128)} %bitcast.1), calls=%async_computation | async-start | bytes 1310720 | tf_op jit(solution)/shard_map/all_to_all | solution.py:314
  42.6 0.7 dynamic-slice_bitcast_fusion
  43.3 0.1 broadcast_in_dim.3
  43.4 0.1 add.39
  43.5 0.0 copy-done.6
  43.5 0.1 fusion.1.refs_1_
  43.6 23.1 %all-to-all-done = f32[1280,1,128]{2,1,0:T(1,128)S(1)} async-done(((f32[1280,1,128]{2,1,0:T(1,128)}), f32[1280,1,128]{2,1,0:T(1,128)S(1)}, u32[]{:S(2)}, u32[]{:S(2)}) %all-to-all-start) | async-done | bytes 655392 | tf_op jit(solution)/shard_map/all_to_all | solution.py:314
  66.7 1.6 %shard_map.99 = f32[1280,128]{1,0:T(8,128)S(1)} custom-call(f32[1280,128]{1,0:T(8,128)S(1)} %bitcast.11, f32[8,128]{1,0:T(8,128)S(1)} %fusion.1.refs_1_, bf16[512,512]{1,0:T(8,128)(2,1)S(1)} %copy-done.3, bf16[512,512]{1,0:T(8,128)(2,1)S(1)} %copy-done.4), custom_call_target="tpu_custom_call" | custom-call | flops 700000000 | bytes 2363392 | tf_op jit(solution)/shard_map/pallas_call | solution.py:55
  68.3 29.7 %all_to_all.10 = f32[1280,1,128]{2,1,0:T(1,128)S(1)} all-to-all(f32[1280,1,128]{2,1,0:T(1,128)S(1)} %bitcast.12), channel_id=1, replica_groups=mesh['gz'=64,'ma'=4] {'gz','ma'}, dimensions={0} | all-to-all | bytes 1310720 | tf_op jit(solution)/shard_map/all_to_all | solution.py:314
  98.0 1.8 %shard_map.100 = (f32[3,1,128,512]{3,2,1,0:T(8,128)}, f32[1,128,512]{2,1,0:T(8,128)}) custom-call(f32[1280,128]{1,0:T(8,128)S(1)} %bitcast.10, f32[3,128,512]{2,1,0:T(8,128)S(1)} %get-tuple-element.13.u, bf16[512,512]{1,0:T(8,128)(2,1)S(1)} %copy-done.3, bf16[512,512]{1,0:T(8,128)(2,1)S(1)} %copy-done.4), custom_call_target="tpu_custom_call" | custom-call | flops 500000000 | bytes 3538944 | tf_op jit(solution)/shard_map/pallas_call | solution.py:55
  (1 shorter events, 0.0 us)
Async XLA Ops:
  0.6 9.2 %collective-permute-start.2 = (s32[1,128,512]{2,1,0:T(8,128)}, s32[1,128,512]{2,1,0:T(8,128)S(1)}, u32[]{:S(2)}, u32[]{:S(2)}) collective-permute-start(s32[1,128,512]{2,1,0:T(8,128)} %phase.1), channel_id=1, source_target_pairs={{4,8},{12,16},{20,24},{28,32},{36,40},{44,48},{52,56},{60,64},{68,... | collective-permute-start | bytes 786440 | tf_op jit(solution)/shard_map/ppermute | solution.py:272
  5.6 4.3 %collective-permute-start.3 = (s32[1,128,512]{2,1,0:T(8,128)}, s32[1,128,512]{2,1,0:T(8,128)S(1)}, u32[]{:S(2)}, u32[]{:S(2)}) collective-permute-start(s32[1,128,512]{2,1,0:T(8,128)} %phase.1), channel_id=1, source_target_pairs={{0,4},{8,12},{16,20},{24,28},{32,36},{40,44},{48,52},{56,60},{64,6... | collective-permute-start | bytes 786440 | tf_op jit(solution)/shard_map/ppermute | solution.py:272
  5.7 1.4 %copy-start = (f32[6,1,128,512]{3,2,1,0:T(8,128)S(1)}, f32[6,1,128,512]{3,2,1,0:T(8,128)}, u32[]{:S(2)}) copy-start(f32[6,1,128,512]{3,2,1,0:T(8,128)} %stress.5) | copy-start | bytes 4718596
  7.1 1.1 %copy-start.1 = (f32[3,1,128,512]{3,2,1,0:T(8,128)S(1)}, f32[3,1,128,512]{3,2,1,0:T(8,128)}, u32[]{:S(2)}) copy-start(f32[3,1,128,512]{3,2,1,0:T(8,128)} %pred_.5) | copy-start | bytes 2359300
  8.2 0.9 copy-start.2
  9.8 6.7 %copy-start.5 = (s32[1,128,512]{2,1,0:T(8,128)S(1)}, s32[1,128,512]{2,1,0:T(8,128)}, u32[]{:S(2)}) copy-start(s32[1,128,512]{2,1,0:T(8,128)} %phase.1) | copy-start | bytes 786436
  10.1 13.3 %collective-permute-start.4 = (f32[3,128,512]{2,1,0:T(8,128)S(1)}, f32[3,128,512]{2,1,0:T(8,128)S(1)}, u32[]{:S(2)}, u32[]{:S(2)}) collective-permute-start(f32[3,128,512]{2,1,0:T(8,128)S(1)} %get-tuple-element.10), channel_id=1, source_target_pairs={{4,8},{12,16},{20,24},{28,32},{36,40},{44,48},{52,56},{60,64},{68,... | collective-permute-start | bytes 2359304 | tf_op jit(solution)/shard_map/ppermute | solution.py:272
  13.8 9.7 %collective-permute-start.5 = (f32[3,128,512]{2,1,0:T(8,128)S(1)}, f32[3,128,512]{2,1,0:T(8,128)S(1)}, u32[]{:S(2)}, u32[]{:S(2)}) collective-permute-start(f32[3,128,512]{2,1,0:T(8,128)S(1)} %get-tuple-element.11), channel_id=1, source_target_pairs={{0,4},{8,12},{16,20},{24,28},{32,36},{40,44},{48,52},{56,60},{64,6... | collective-permute-start | bytes 2359304 | tf_op jit(solution)/shard_map/ppermute | solution.py:272
  13.9 2.7 %collective-permute-start = (f32[8,512]{1,0:T(8,128)S(1)}, f32[8,512]{1,0:T(8,128)S(1)}, u32[]{:S(2)}, u32[]{:S(2)}) collective-permute-start(f32[8,512]{1,0:T(8,128)S(1)} %get-tuple-element.8._), channel_id=1, source_target_pairs={{0,1},{2,3},{1,0},{3,2},{4,5},{6,7},{5,4},{7,6},{8,9},{10,11},{9,8... | collective-permute-start | bytes 49160 | tf_op jit(solution)/shard_map/ppermute | solution.py:272
  15.2 8.3 %copy-start.3 = (bf16[512,512]{1,0:T(8,128)(2,1)S(1)}, bf16[512,512]{1,0:T(8,128)(2,1)}, u32[]{:S(2)}) copy-start(bf16[512,512]{1,0:T(8,128)(2,1)} %constant.31.clone.high.refs_2_) | copy-start | bytes 1572868
  15.2 8.3 %copy-start.4 = (bf16[512,512]{1,0:T(8,128)(2,1)S(1)}, bf16[512,512]{1,0:T(8,128)(2,1)}, u32[]{:S(2)}) copy-start(bf16[512,512]{1,0:T(8,128)(2,1)} %constant.32.clone.low.refs_3_) | copy-start | bytes 1572868
  15.2 1.4 %collective-permute-start.1 = (f32[8,512]{1,0:T(8,128)S(1)}, f32[8,512]{1,0:T(8,128)S(1)}, u32[]{:S(2)}, u32[]{:S(2)}) collective-permute-start(f32[8,512]{1,0:T(8,128)S(1)} %get-tuple-element.9), channel_id=1, source_target_pairs={{1,2},{2,1},{5,6},{6,5},{9,10},{10,9},{13,14},{14,13},{17,18},{18,... | collective-permute-start | bytes 49160 | tf_op jit(solution)/shard_map/ppermute | solution.py:272
  17.8 25.7 %copy-start.6 = (f32[8,128]{1,0:T(8,128)S(1)}, f32[8,128]{1,0:T(8,128)}, u32[]{:S(2)}) copy-start(f32[8,128]{1,0:T(8,128)} %constant.39) | copy-start | bytes 12292
  25.9 40.9 %all-to-all-start = ((f32[1280,1,128]{2,1,0:T(1,128)}), f32[1280,1,128]{2,1,0:T(1,128)S(1)}, u32[]{:S(2)}, u32[]{:S(2)}) async-start(f32[1280,1,128]{2,1,0:T(1,128)} %bitcast.1), calls=%async_computation | async-start | bytes 1310720 | tf_op jit(solution)/shard_map/all_to_all | solution.py:314

commit v2 on v1

--- a/solution.py
+++ b/solution.py
@@ -49,18 +49,22 @@
     return pl.BlockSpec(memory_space=pltpu.VMEM)
 
 
-def call(body, outs, args, flops, scratch=()):
+def call(body, outs, args, flops, scratch=(), out_space=pltpu.VMEM):
     shapes = [jax.ShapeDtypeStruct(shape, F32) for shape in outs]
     moved = sum(a.size * a.dtype.itemsize for a in args) + sum(4 * s.size for s in shapes)
     return pl.pallas_call(
         body,
         out_shape=shapes,
         in_specs=[whole() for _ in args],
-        out_specs=[whole() for _ in outs],
+        out_specs=[pl.BlockSpec(memory_space=out_space) for _ in outs],
         scratch_shapes=list(scratch),
         cost_estimate=pl.CostEstimate(flops=flops, bytes_accessed=moved, transcendentals=0),
         compiler_params=pltpu.CompilerParams(vmem_limit_bytes=VMEM_LIMIT),
     )(*args)
+
+
+def near_sign():
+    return jnp.where(lax.axis_index("gz") % 2 == 1, F32(1), F32(-1))
 
 
 def rows_body(pred, stress, old, even_row, odd_row):
@@ -74,18 +78,6 @@
         odd_row[i : i + 1] = jnp.where(even, low, high)
     even_row[7:8] = jnp.zeros_like(even_row[7:8])
     odd_row[7:8] = jnp.zeros_like(odd_row[7:8])
-
-
-def send_body(pred, stress, old, far_phase, near_phase, _, far, near):
-    odd = lax.axis_index("gz") % 2 == 1
-    far_sign = jnp.where(odd, F32(-1), F32(1))
-    for out, phase, sign in ((far, far_phase, far_sign), (near, near_phase, -far_sign)):
-        liquid = phase[0] == 1
-        half = jnp.where(liquid, sign * STRESS_LIQUID, sign * STRESS_GAS)
-        out[0] = VISCOUS * pred[0, 0] + half * stress[4, 0]
-        out[1] = VISCOUS * pred[1, 0] + half * stress[5, 0]
-        push = jnp.where(liquid, sign * OLD_LIQUID, 0.0)
-        out[2] = VISCOUS * pred[2, 0] + half * stress[2, 0] + push * old[0]
 
 
 def shifted(value, low_row=None, high_row=None):
@@ -106,7 +98,37 @@
     return below, above
 
 
-def local_body(pred, stress, phase, old, even_row, odd_row, out):
+def for_far(pred, stress, phase):
+    sign = -near_sign()
+    half = jnp.where(phase[0] == 1, sign * STRESS_LIQUID, sign * STRESS_GAS)
+    add_x = VISCOUS * pred[0, 0] + half * stress[4, 0]
+    return add_x, VISCOUS * pred[1, 0] + half * stress[5, 0]
+
+
+def send_body(pred, stress, old, phase, _, far, near):
+    rows = old.shape[1]
+    sign = -near_sign()
+    add_x, add_y = for_far(pred, stress, phase)
+    behind, ahead = shifted(add_x)
+    left, right = shifted_y(add_y)
+    far[0:rows] = (ahead - behind) + (right - left)
+    liquid = sign * (STRESS_LIQUID * stress[2, 0] + OLD_LIQUID * old[0])
+    gas = (sign * STRESS_GAS) * stress[2, 0]
+    viscous = VISCOUS * pred[2, 0]
+    far[rows : 2 * rows] = viscous + jnp.where(phase[0] == 1, liquid, gas)
+    far[2 * rows : 2 * rows + 1] = add_x[0:1]
+    far[2 * rows + 1 : 2 * rows + 2] = add_x[rows - 1 : rows]
+    far[2 * rows + 2 : 2 * rows + 8] = jnp.zeros((6, old.shape[2]), F32)
+    near[0] = VISCOUS * pred[0, 0]
+    near[1] = -sign * stress[4, 0]
+    near[2] = VISCOUS * pred[1, 0]
+    near[3] = -sign * stress[5, 0]
+    near[4] = viscous - liquid
+    near[5] = viscous - gas
+
+
+def local_body(pred, stress, phase, old, even_row, odd_row, far_phase, out, later):
+    later[0], later[1] = for_far(pred, stress, far_phase)
     even = lax.axis_index("ma") % 2 == 0
     before = jnp.where(even, odd_row[...], even_row[...])
     after = jnp.where(even, even_row[...], odd_row[...])
@@ -141,38 +163,44 @@
         out[i] = total
 
 
-def source_body(local, far, near, high, low, out, sent):
-    u_x = local[0] + (far[0] + near[0])
-    u_y = local[1] + (far[1] + near[1])
-    u_z = local[2] + (far[2] + near[2])
+def source_body(local, far, near, phase, high, low, out, sent):
+    liquid = phase[0] == 1
+    half = jnp.where(liquid, STRESS_LIQUID, STRESS_GAS)
+    rows = local.shape[1]
+    u_x = local[0] + (near[0] + half * near[1])
+    u_y = local[1] + (near[2] + half * near[3])
+    u_z = local[2] + far[rows : 2 * rows] + jnp.where(liquid, near[4], near[5])
     out[0], out[1], out[2] = u_x, u_y, u_z
     behind, ahead = shifted(u_x)
     left, right = shifted_y(u_y)
-    planar = (ahead - behind) + (right - left)
-    table = (high[...], low[...])
-    nt = ((1,), (1,))
+    planar = (ahead - behind) + (right - left) + far[0:rows]
+    spot = lax.broadcasted_iota(jnp.int32, u_x.shape, 0)
+    first = u_x[0:1] + far[2 * rows : 2 * rows + 1]
+    last = u_x[rows - 1 : rows] + far[2 * rows + 1 : 2 * rows + 2]
+    ends = jnp.where(spot == 0, first, jnp.where(spot == 1, last, 0.0))
+    fields = split(jnp.concatenate([planar, u_z, ends], 0))
+    modes = product_3((high[...], low[...]), fields, ((1,), (1,)))
     pairs = sent.shape[0] // 5
-    for i, value in enumerate((planar, u_z)):
-        modes = product_3(table, split(value), nt)
-        sent[pl.ds(2 * i, pairs, 5)] = modes[:pairs]
-        sent[pl.ds(2 * i + 1, pairs, 5)] = modes[pairs:]
-    rows, columns = u_x.shape
-    first, last = u_x[0:1], u_x[rows - 1 : rows]
-    spot = lax.broadcasted_iota(jnp.int32, (128, columns), 0)
-    zero = jnp.zeros((128, columns), F32)
-    lead = jnp.where(spot == 0, first, jnp.where(spot == 1, last, zero))
-    trail = jnp.where(spot == 2, first, jnp.where(spot == 3, last, zero))
-    ends = product_3((high[:pairs], low[:pairs]), split(lead), nt)
-    ends = ends + product_3((high[pairs:], low[pairs:]), split(trail), nt)
-    sent[pl.ds(4, pairs, 5)] = ends
-
-
-def solve_body(blocks, received, ratio, high, low, sent, held, result):
+    for i in range(2):
+        for j in range(2):
+            sent[pl.ds(2 * i + j, pairs, 5)] = modes[
+                j * pairs : (j + 1) * pairs, i * rows : (i + 1) * rows
+            ]
+    ends = modes[:, 2 * rows : 3 * rows]
+    sent[pl.ds(4, pairs, 5)] = ends[:pairs] + pltpu.roll(ends[pairs:], 2, 1)
+
+
+def solve_body(blocks, received, part_x, part_y, high, low, sent, held, result):
     planes = received.shape[0] // (5 * blocks)
     step = 5 * blocks
-    tiles = ratio.shape[0] // 2
+    tiles = part_x.shape[0] // 2
     lane = lax.broadcasted_iota(jnp.int32, (planes, 128), 1)
     row = lax.broadcasted_iota(jnp.int32, (planes, 128), 0)
+    own = lax.axis_index("gz") * blocks + lax.axis_index("ma")
+    mine = lax.broadcasted_iota(jnp.int32, part_y.shape, 1) == own
+    wave_y = jnp.sum(jnp.where(mine, part_y[...], 0.0), axis=1, keepdims=True)
+    spread = SHIFT_TERM + part_x[...] + wave_y
+    r = 2.0 / (2.0 + spread + jnp.sqrt(spread * (spread + 4.0)))
     ends = [received[pl.ds(5 * b + 4, planes, step)] for b in range(blocks)]
     sides = []
     for j in range(2):
@@ -196,7 +224,6 @@
             held[pl.ds(j * tiles + t, planes, every)] = modes[
                 j * planes : (j + 1) * planes, t * 128 : (t + 1) * 128
             ]
-    r = ratio[...]
     carry = jnp.zeros_like(r)
     for z in range(planes):
         carry = r * (carry - held[every * z : every * (z + 1)])
@@ -237,26 +264,33 @@
         sent[pl.ds(5 * b + 4, planes, step)] = edge
 
 
-def final_body(received, u, high, low, velocity, pressure):
+def final_body(received, u, later, high, low, velocity, pressure, made, arrived):
     pairs = received.shape[0] // 5
     table = (high[...], low[...])
     nn = ((1,), (0,))
+    places = (velocity.at[0, 0], velocity.at[1, 0], velocity.at[2, 0], pressure.at[0])
+    copies = [pltpu.make_async_copy(made.at[i], places[i], arrived.at[i]) for i in range(4)]
 
     def field(i):
         pieces = [received[pl.ds(i + j, pairs, 5)] for j in range(2)]
         return product_3(split(jnp.concatenate(pieces, 0).T), table, nn)
 
+    made[2] = u[2] - 0.25 * field(2)
+    copies[2].start()
     p = field(0)
-    along_z = field(2)
+    made[3] = p
+    copies[3].start()
+    left, right = shifted_y(p)
+    made[1] = u[1] + later[1] - 0.25 * (right - left)
+    copies[1].start()
     ends = split(received[pl.ds(4, pairs, 5)].T[0:8])
     lead = product_3(ends, (high[:pairs], low[:pairs]), nn)
     trail = product_3(ends, (high[pairs:], low[pairs:]), nn)
     behind, ahead = shifted(p, lead[0:1] + trail[2:3], lead[1:2] + trail[3:4])
-    left, right = shifted_y(p)
-    pressure[0] = p
-    velocity[0, 0] = u[0] - 0.25 * (ahead - behind)
-    velocity[1, 0] = u[1] - 0.25 * (right - left)
-    velocity[2, 0] = u[2] - 0.25 * along_z
+    made[0] = u[0] + later[0] - 0.25 * (ahead - behind)
+    copies[0].start()
+    for copy in copies:
+        copy.wait()
 
 
 def shards(predictor, stress, phase, old_pressure):
@@ -272,52 +306,46 @@
         return lax.ppermute(value, axis, pairs + [(b, a) for a, b in pairs])
 
     far_phase = swap(phase, "gz", 1)
-    near_phase = swap(phase, "gz", 0)
     even_row, odd_row = call(
         rows_body, [(8, columns), (8, columns)], (predictor, stress, old_pressure), 10000
     )
     far, near = call(
         send_body,
-        [(3, rows, columns), (3, rows, columns)],
-        (predictor, stress, old_pressure, far_phase, near_phase, even_row),
+        [(2 * rows + 8, columns), (6, rows, columns)],
+        (predictor, stress, old_pressure, far_phase, even_row),
         1000000,
     )
+    far = swap(far, "gz", 1)
+    near = swap(near, "gz", 0)
     even_row = swap(even_row, "ma", 0)
     odd_row = swap(odd_row, "ma", 1)
-    far = swap(far, "gz", 1)
-    near = swap(near, "gz", 0)
-
-    own = lax.axis_index("gz") * lines + lax.axis_index("ma")
-    tiles = columns // 128
-    part_x = jnp.asarray(np.tile(eigen.reshape(tiles, 128), (2, 1)))
-    pair = lax.dynamic_index_in_dim(
-        jnp.asarray(eigen.reshape(2, devices)), own, 1, keepdims=False
-    )
-    part_y = jnp.repeat(pair, tiles)[:, None]
-    spread = SHIFT_TERM + part_x + part_y
-    ratio = 2.0 / (2.0 + spread + jnp.sqrt(spread * (spread + 4.0)))
-
-    (local,) = call(
+
+    local, later = call(
         local_body,
-        [(3, rows, columns)],
-        (predictor, stress, phase, old_pressure, even_row, odd_row),
+        [(3, rows, columns), (2, rows, columns)],
+        (predictor, stress, phase, old_pressure, even_row, odd_row, far_phase),
         8000000,
     )
+    later = swap(later, "gz", 1)
     u, modes = call(
         source_body,
         [(3, rows, columns), (5 * devices, 128)],
-        (local, far, near, high, low),
+        (local, far, near, phase, high, low),
         600000000,
     )
 
     def exchange(value):
-        moved = lax.all_to_all(value.reshape(5 * devices, 1, 128), ("gz", "ma"), 0, 0, tiled=True)
-        return moved.reshape(5 * devices, 128)
-
+        count = value.shape[0]
+        moved = lax.all_to_all(value.reshape(count, 1, 128), ("gz", "ma"), 0, 0, tiled=True)
+        return moved.reshape(count, 128)
+
+    tiles = columns // 128
+    part_x = jnp.asarray(np.tile(eigen.reshape(tiles, 128), (2, 1)))
+    part_y = jnp.asarray(np.repeat(eigen.reshape(2, devices), tiles, axis=0))
     (solved,) = call(
         lambda *refs: solve_body(lines, *refs),
         [(5 * devices, 128)],
-        (exchange(modes), ratio, high, low),
+        (exchange(modes), part_x, part_y, high, low),
         700000000,
         (
             pltpu.VMEM((2 * tiles * planes_z, 128), F32),
@@ -327,8 +355,10 @@
     velocity, pressure = call(
         final_body,
         [(3, 1, rows, columns), (1, rows, columns)],
-        (exchange(solved), u, high, low),
+        (exchange(solved), u, later, high, low),
         500000000,
+        (pltpu.VMEM((4, rows, columns), F32), pltpu.SemaphoreType.DMA((4,))),
+        pl.ANY,
     )
     return velocity, pressure
 

time: 100 us -> 97.4 us (0.974)
  blocking collectives: 29.7 us -> 40.2 us
  waiting for transfers between devices: 30 us -> 22.1 us
  starting transfers between devices: 27.6 us -> 23.1 us
    all_to_all x1, waiting for transfers between devices: 23.1 us -> 3.19 us  [exchange(): lax.all_to_all(value.reshape(count, 1, 128), ('gz', 'ma'), 0, 0, tiled=True)]
    ppermute x6, waiting for transfers between devices: 6.89 us -> 18.9 us  [swap(): return lax.ppermute(value, axis, pairs + [(b, a) for a, b in pairs])]
    all_to_all x1, starting transfers between devices: 16.8 us -> 5.8 us  [exchange(): lax.all_to_all(value.reshape(count, 1, 128), ('gz', 'ma'), 0, 0, tiled=True)]
    all_to_all x1, blocking collectives: 29.7 us -> 40.2 us  [exchange(): lax.all_to_all(value.reshape(count, 1, 128), ('gz', 'ma'), 0, 0, tiled=True)]
    ppermute x6, starting transfers between devices: 10.8 us -> 17.3 us  [swap(): return lax.ppermute(value, axis, pairs + [(b, a) for a, b in pairs])]
    unnamed x14 -> x16, local copies, waits for them, and re-layouts: 3.5 us -> 3.52 us
  transfers between devices with their start and end apart: 7 -> 7, of which waited for: 4 -> 4; matrix products, arithmetic and copies ran while one was open for 1% -> 0% of each run, Pallas kernels for 1% -> 1%
where the time goes in v2:
time: 97.4 us; the launch traced here: 97 us
  blocking collectives  40.2 us (41%)
  starting transfers between devices  23.1 us (24%)
  waiting for transfers between devices  22.1 us (23%)
  Pallas kernels  7.23 us (7%)
  local copies, waits for them, and re-layouts  3.52 us (4%)
    all_to_all x1, blocking collectives, exchange(): lax.all_to_all(value.reshape(count, 1, 128), ('gz', 'ma'), 0, 0, tiled=True)  40.2 us
    ppermute x6, waiting for transfers between devices, swap(): return lax.ppermute(value, axis, pairs + [(b, a) for a, b in pairs])  18.9 us
    ppermute x6, starting transfers between devices, swap(): return lax.ppermute(value, axis, pairs + [(b, a) for a, b in pairs])  17.3 us
    pallas_call x6, Pallas kernels, call(): pl.pallas_call(body, out_shape=shapes, in_specs=[whole() for _ in args],...  7.23 us
    all_to_all x1, starting transfers between devices, exchange(): lax.all_to_all(value.reshape(count, 1, 128), ('gz', 'ma'), 0, 0, tiled=True)  5.8 us
    unnamed x16, local copies, waits for them, and re-layouts  3.52 us
    all_to_all x1, waiting for transfers between devices, exchange(): lax.all_to_all(value.reshape(count, 1, 128), ('gz', 'ma'), 0, 0, tiled=True)  3.19 us
  transfers between devices with their start and end apart: 7, of which 4 were waited for; matrix products, arithmetic and copies ran while one was open for 0% of the time, Pallas kernels for 1%

profile of v2, /device:TPU:1, one launch (start us, length us, event | category | flops | bytes accessed | tf_op | source)
XLA Modules:
  0.0 97.0 jit_solution(3103243542904657905)
XLA Ops:
  0.6 4.9 %collective-permute-start.2 = (s32[1,128,512]{2,1,0:T(8,128)}, s32[1,128,512]{2,1,0:T(8,128)S(1)}, u32[]{:S(2)}, u32[]{:S(2)}) collective-permute-start(s32[1,128,512]{2,1,0:T(8,128)} %phase.3), channel_id=1, source_target_pairs={{4,8},{12,16},{20,24},{28,32},{36,40},{44,48},{52,56},{60,64},{68,... | collective-permute-start | bytes 786440 | tf_op jit(solution)/shard_map/ppermute | solution.py:306
  5.6 0.0 copy-start
  5.6 1.4 %copy-done = f32[6,1,128,512]{3,2,1,0:T(8,128)S(1)} copy-done((f32[6,1,128,512]{3,2,1,0:T(8,128)S(1)}, f32[6,1,128,512]{3,2,1,0:T(8,128)}, u32[]{:S(2)}) %copy-start) | copy-done | bytes 1572888
  7.0 0.0 copy-start.1
  7.0 1.1 %copy-done.1 = f32[3,1,128,512]{3,2,1,0:T(8,128)S(1)} copy-done((f32[3,1,128,512]{3,2,1,0:T(8,128)S(1)}, f32[3,1,128,512]{3,2,1,0:T(8,128)}, u32[]{:S(2)}) %copy-start.1) | copy-done | bytes 786456
  8.1 0.0 copy-start.2
  8.1 0.9 copy-done.2
  9.1 0.0 copy-start.5
  9.1 0.7 collective-permute-done.2.far_phase.phase
  9.8 0.5 shard_map.97
  10.3 0.1 collective-permute-start.4
  10.4 3.9 %collective-permute-start.3 = (f32[264,512]{1,0:T(8,128)S(1)}, f32[264,512]{1,0:T(8,128)S(1)}, u32[]{:S(2)}, u32[]{:S(2)}) collective-permute-start(f32[264,512]{1,0:T(8,128)S(1)} %get-tuple-element.13), channel_id=1, source_target_pairs={{4,8},{12,16},{20,24},{28,32},{36,40},{44,48},{52,56},{60,64},{68,... | collective-permute-start | bytes 1622024 | tf_op jit(solution)/shard_map/ppermute | solution.py:306
  14.3 0.0 copy-start.3
  14.4 0.0 copy-start.4
  14.4 0.8 collective-permute-start.1
  15.2 3.8 %collective-permute-start = (f32[8,512]{1,0:T(8,128)S(1)}, f32[8,512]{1,0:T(8,128)S(1)}, u32[]{:S(2)}, u32[]{:S(2)}) collective-permute-start(f32[8,512]{1,0:T(8,128)S(1)} %get-tuple-element.10._), channel_id=1, source_target_pairs={{0,1},{2,3},{1,0},{3,2},{4,5},{6,7},{5,4},{7,6},{8,9},{10,11},{9,8... | collective-permute-start | bytes 49160 | tf_op jit(solution)/shard_map/ppermute | solution.py:306
  18.9 0.0 collective-permute-done.1.odd_row
  18.9 1.1 %collective-permute-done.even_row = f32[8,512]{1,0:T(8,128)S(1)} collective-permute-done((f32[8,512]{1,0:T(8,128)S(1)}, f32[8,512]{1,0:T(8,128)S(1)}, u32[]{:S(2)}, u32[]{:S(2)}) %collective-permute-start) | collective-permute-done | bytes 16416 | tf_op jit(solution)/shard_map/ppermute | solution.py:306
  20.1 0.0 copy-done.5
  20.1 1.4 %shard_map.96 = (f32[3,128,512]{2,1,0:T(8,128)S(1)}, f32[2,128,512]{2,1,0:T(8,128)S(1)}) custom-call(f32[3,1,128,512]{3,2,1,0:T(8,128)S(1)} %copy-done.1, f32[6,1,128,512]{3,2,1,0:T(8,128)S(1)} %copy-done, s32[1,128,512]{2,1,0:T(8,128)S(1)} %copy-done.5, f32[1,128,512]{2,1,0:T(8,128)S(1)} %copy-done.2, f32[8,512]{1,0:T(8,128)S(1)} %collective-permute-done.even_row, ...), custom_call_target="tpu_custom_call" | custom-call | flops 8000000 | bytes 4489216 | tf_op jit(solution)/shard_map/pallas_call | solution.py:55
  21.5 0.0 collective-permute-done.3.far
  21.5 0.0 collective-permute-done.4.near
  21.5 0.0 copy-done.3
  21.5 0.0 copy-done.4
  21.5 0.0 copy-start.6
  21.5 0.0 copy-start.7
  21.5 1.2 %shard_map.98 = (f32[3,128,512]{2,1,0:T(8,128)S(1)}, f32[1280,128]{1,0:T(8,128)S(1)}) custom-call(f32[3,128,512]{2,1,0:T(8,128)S(1)} %get-tuple-element.12.local, f32[264,512]{1,0:T(8,128)S(1)} %collective-permute-done.3.far, f32[6,128,512]{2,1,0:T(8,128)S(1)} %collective-permute-done.4.near, s32[1,128,512]{2,1,0:T(8,128)S(1)} %copy-done.5, ...), custom_call_target="tpu_custom_call" | custom-call | flops 600000000 | bytes 5652480 | tf_op jit(solution)/shard_map/pallas_call | solution.py:55
  22.8 40.2 %all_to_all.10 = f32[1280,1,128]{2,1,0:T(1,128)S(1)} all-to-all(f32[1280,1,128]{2,1,0:T(1,128)S(1)} %bitcast.9), channel_id=1, replica_groups=mesh['gz'=64,'ma'=4] {'gz','ma'}, dimensions={0} | all-to-all | bytes 1310720 | tf_op jit(solution)/shard_map/all_to_all | solution.py:339
  63.0 0.0 copy-done.6
  63.0 0.0 copy-done.7
  63.0 2.4 %shard_map.99 = f32[1280,128]{1,0:T(8,128)} custom-call(f32[1280,128]{1,0:T(8,128)S(1)} %bitcast.10, f32[8,128]{1,0:T(8,128)S(1)} %copy-done.7, f32[8,256]{1,0:T(8,128)S(1)} %copy-done.6, bf16[512,512]{1,0:T(8,128)(2,1)S(1)} %copy-done.4, bf16[512,512]{1,0:T(8,128)(2,1)S(1)} %copy-done.3), custom_call_target="tpu_custom_call" | custom-call | flops 700000000 | bytes 2371584 | tf_op jit(solution)/shard_map/pallas_call | solution.py:55
  65.5 5.8 %all-to-all-start.1 = ((f32[1280,1,128]{2,1,0:T(1,128)}), f32[1280,1,128]{2,1,0:T(1,128)S(1)}, u32[]{:S(2)}, u32[]{:S(2)}) async-start(f32[1280,1,128]{2,1,0:T(1,128)} %bitcast.4), calls=%async_computation.1 | async-start | bytes 1310720 | tf_op jit(solution)/shard_map/all_to_all | solution.py:339
  71.3 3.8 %collective-permute-start.5 = (f32[2,128,512]{2,1,0:T(8,128)S(1)}, f32[2,128,512]{2,1,0:T(8,128)S(1)}, u32[]{:S(2)}, u32[]{:S(2)}) collective-permute-start(f32[2,128,512]{2,1,0:T(8,128)S(1)} %get-tuple-element.17), channel_id=1, source_target_pairs={{4,8},{12,16},{20,24},{28,32},{36,40},{44,48},{52,56},{60,64},{68,... | collective-permute-start | bytes 1572872 | tf_op jit(solution)/shard_map/ppermute | solution.py:306
  75.1 17.1 %collective-permute-done.5.later = f32[2,128,512]{2,1,0:T(8,128)S(1)} collective-permute-done((f32[2,128,512]{2,1,0:T(8,128)S(1)}, f32[2,128,512]{2,1,0:T(8,128)S(1)}, u32[]{:S(2)}, u32[]{:S(2)}) %collective-permute-start.5) | collective-permute-done | bytes 524320 | tf_op jit(solution)/shard_map/ppermute | solution.py:306
  92.1 3.2 %all-to-all-done.1 = f32[1280,1,128]{2,1,0:T(1,128)S(1)} async-done(((f32[1280,1,128]{2,1,0:T(1,128)}), f32[1280,1,128]{2,1,0:T(1,128)S(1)}, u32[]{:S(2)}, u32[]{:S(2)}) %all-to-all-start.1) | async-done | bytes 655392 | tf_op jit(solution)/shard_map/all_to_all | solution.py:339
  95.3 1.7 %shard_map.100 = (f32[3,1,128,512]{3,2,1,0:T(8,128)}, f32[1,128,512]{2,1,0:T(8,128)}) custom-call(f32[1280,128]{1,0:T(8,128)S(1)} %bitcast.8, f32[3,128,512]{2,1,0:T(8,128)S(1)} %get-tuple-element.16.u, f32[2,128,512]{2,1,0:T(8,128)S(1)} %collective-permute-done.5.later, bf16[512,512]{1,0:T(8,128)(2,1)S(1)} %copy-done.4, bf16[512,512]{1,0:T(8,128)(2,1)S(1)} %copy-done.3), custom_call_target="tpu_custom_call" | custom-call | flops 500000000 | bytes 4063232 | tf_op jit(solution)/shard_map/pallas_call | solution.py:55
  (1 shorter events, 0.0 us)
Async XLA Ops:
  0.6 9.2 %collective-permute-start.2 = (s32[1,128,512]{2,1,0:T(8,128)}, s32[1,128,512]{2,1,0:T(8,128)S(1)}, u32[]{:S(2)}, u32[]{:S(2)}) collective-permute-start(s32[1,128,512]{2,1,0:T(8,128)} %phase.3), channel_id=1, source_target_pairs={{4,8},{12,16},{20,24},{28,32},{36,40},{44,48},{52,56},{60,64},{68,... | collective-permute-start | bytes 786440 | tf_op jit(solution)/shard_map/ppermute | solution.py:306
  5.6 1.4 %copy-start = (f32[6,1,128,512]{3,2,1,0:T(8,128)S(1)}, f32[6,1,128,512]{3,2,1,0:T(8,128)}, u32[]{:S(2)}) copy-start(f32[6,1,128,512]{3,2,1,0:T(8,128)} %stress.5) | copy-start | bytes 4718596
  7.0 1.1 %copy-start.1 = (f32[3,1,128,512]{3,2,1,0:T(8,128)S(1)}, f32[3,1,128,512]{3,2,1,0:T(8,128)}, u32[]{:S(2)}) copy-start(f32[3,1,128,512]{3,2,1,0:T(8,128)} %pred_.5) | copy-start | bytes 2359300
  8.1 0.9 copy-start.2
  9.1 11.0 %copy-start.5 = (s32[1,128,512]{2,1,0:T(8,128)S(1)}, s32[1,128,512]{2,1,0:T(8,128)}, u32[]{:S(2)}) copy-start(s32[1,128,512]{2,1,0:T(8,128)} %phase.3) | copy-start | bytes 786436
  10.3 11.2 %collective-permute-start.4 = (f32[6,128,512]{2,1,0:T(8,128)S(1)}, f32[6,128,512]{2,1,0:T(8,128)S(1)}, u32[]{:S(2)}, u32[]{:S(2)}) collective-permute-start(f32[6,128,512]{2,1,0:T(8,128)S(1)} %get-tuple-element.14), channel_id=1, source_target_pairs={{0,4},{8,12},{16,20},{24,28},{32,36},{40,44},{48,52},{56,60},{64,6... | collective-permute-start | bytes 4718600 | tf_op jit(solution)/shard_map/ppermute | solution.py:306
  10.4 11.1 %collective-permute-start.3 = (f32[264,512]{1,0:T(8,128)S(1)}, f32[264,512]{1,0:T(8,128)S(1)}, u32[]{:S(2)}, u32[]{:S(2)}) collective-permute-start(f32[264,512]{1,0:T(8,128)S(1)} %get-tuple-element.13), channel_id=1, source_target_pairs={{4,8},{12,16},{20,24},{28,32},{36,40},{44,48},{52,56},{60,64},{68,... | collective-permute-start | bytes 1622024 | tf_op jit(solution)/shard_map/ppermute | solution.py:306
  14.3 7.2 %copy-start.3 = (bf16[512,512]{1,0:T(8,128)(2,1)S(1)}, bf16[512,512]{1,0:T(8,128)(2,1)}, u32[]{:S(2)}) copy-start(bf16[512,512]{1,0:T(8,128)(2,1)} %constant.9.clone.low.refs_4_) | copy-start | bytes 1572868
  14.4 7.2 %copy-start.4 = (bf16[512,512]{1,0:T(8,128)(2,1)S(1)}, bf16[512,512]{1,0:T(8,128)(2,1)}, u32[]{:S(2)}) copy-start(bf16[512,512]{1,0:T(8,128)(2,1)} %constant.8.clone.high.refs_3_) | copy-start | bytes 1572868
  14.4 4.6 %collective-permute-start.1 = (f32[8,512]{1,0:T(8,128)S(1)}, f32[8,512]{1,0:T(8,128)S(1)}, u32[]{:S(2)}, u32[]{:S(2)}) collective-permute-start(f32[8,512]{1,0:T(8,128)S(1)} %get-tuple-element.11), channel_id=1, source_target_pairs={{1,2},{2,1},{5,6},{6,5},{9,10},{10,9},{13,14},{14,13},{17,18},{18,... | collective-permute-start | bytes 49160 | tf_op jit(solution)/shard_map/ppermute | solution.py:306
  15.2 4.9 %collective-permute-start = (f32[8,512]{1,0:T(8,128)S(1)}, f32[8,512]{1,0:T(8,128)S(1)}, u32[]{:S(2)}, u32[]{:S(2)}) collective-permute-start(f32[8,512]{1,0:T(8,128)S(1)} %get-tuple-element.10._), channel_id=1, source_target_pairs={{0,1},{2,3},{1,0},{3,2},{4,5},{6,7},{5,4},{7,6},{8,9},{10,11},{9,8... | collective-permute-start | bytes 49160 | tf_op jit(solution)/shard_map/ppermute | solution.py:306
  21.5 41.5 %copy-start.6 = (f32[8,256]{1,0:T(8,128)S(1)}, f32[8,256]{1,0:T(8,128)}, u32[]{:S(2)}) copy-start(f32[8,256]{1,0:T(8,128)} %constant.11.clone.refs_2_) | copy-start | bytes 24580
  21.5 41.5 %copy-start.7 = (f32[8,128]{1,0:T(8,128)S(1)}, f32[8,128]{1,0:T(8,128)}, u32[]{:S(2)}) copy-start(f32[8,128]{1,0:T(8,128)} %constant.10.clone.refs_1_) | copy-start | bytes 12292
  65.5 29.9 %all-to-all-start.1 = ((f32[1280,1,128]{2,1,0:T(1,128)}), f32[1280,1,128]{2,1,0:T(1,128)S(1)}, u32[]{:S(2)}, u32[]{:S(2)}) async-start(f32[1280,1,128]{2,1,0:T(1,128)} %bitcast.4), calls=%async_computation.1 | async-start | bytes 1310720 | tf_op jit(solution)/shard_map/all_to_all | solution.py:339
  71.3 20.9 %collective-permute-start.5 = (f32[2,128,512]{2,1,0:T(8,128)S(1)}, f32[2,128,512]{2,1,0:T(8,128)S(1)}, u32[]{:S(2)}, u32[]{:S(2)}) collective-permute-start(f32[2,128,512]{2,1,0:T(8,128)S(1)} %get-tuple-element.17), channel_id=1, source_target_pairs={{4,8},{12,16},{20,24},{28,32},{36,40},{44,48},{52,56},{60,64},{68,... | collective-permute-start | bytes 1572872 | tf_op jit(solution)/shard_map/ppermute | solution.py:306

commit v3 on v2

--- a/solution.py
+++ b/solution.py
@@ -224,16 +224,34 @@
             held[pl.ds(j * tiles + t, planes, every)] = modes[
                 j * planes : (j + 1) * planes, t * 128 : (t + 1) * 128
             ]
-    carry = jnp.zeros_like(r)
-    for z in range(planes):
-        carry = r * (carry - held[every * z : every * (z + 1)])
-        held[every * z : every * (z + 1)] = carry
-    carry = jnp.zeros_like(r)
-    result[0:every] = carry
-    result[every * (planes + 1) : every * (planes + 2)] = carry
-    for z in reversed(range(planes)):
-        carry = r * carry + held[every * z : every * (z + 1)]
-        result[every * (z + 1) : every * (z + 2)] = carry
+    half = planes // 2
+    zero = jnp.zeros_like(r)
+    powers = [r]
+    for _ in range(half - 1):
+        powers.append(powers[-1] * r)
+    carry, other = zero, zero
+    for z in range(half):
+        here = slice(every * z, every * (z + 1))
+        there = slice(every * (z + half), every * (z + half + 1))
+        carry = r * (carry - held[here])
+        other = r * (other - held[there])
+        held[here] = carry
+        held[there] = other
+    for z in range(half):
+        there = slice(every * (z + half), every * (z + half + 1))
+        held[there] = held[there] + powers[z] * carry
+    result[0:every] = zero
+    result[every * (planes + 1) : every * (planes + 2)] = zero
+    carry, other = zero, zero
+    for z in range(half):
+        low, high_z = half - 1 - z, planes - 1 - z
+        carry = r * carry + held[every * high_z : every * (high_z + 1)]
+        other = r * other + held[every * low : every * (low + 1)]
+        result[every * (high_z + 1) : every * (high_z + 2)] = carry
+        result[every * (low + 1) : every * (low + 2)] = other
+    for z in range(half):
+        here = slice(every * (half - z), every * (half - z + 1))
+        result[here] = result[here] + powers[z] * carry
     fields = []
     for j in range(2):
         pieces = [result[pl.ds(every + j * tiles + t, planes, every)] for t in range(tiles)]

time: 97.4 us -> 97.2 us (level)
  no operation moved by 1% of the time
where the time goes in v3:
time: 97.2 us; the launch traced here: 96.9 us
  blocking collectives  40.2 us (41%)
  starting transfers between devices  23.1 us (24%)
  waiting for transfers between devices  22.1 us (23%)
  Pallas kernels  7.1 us (7%)
  local copies, waits for them, and re-layouts  3.52 us (4%)
    all_to_all x1, blocking collectives, exchange(): lax.all_to_all(value.reshape(count, 1, 128), ('gz', 'ma'), 0, 0, tiled=True)  40.2 us
    ppermute x6, waiting for transfers between devices, swap(): return lax.ppermute(value, axis, pairs + [(b, a) for a, b in pairs])  18.9 us
    ppermute x6, starting transfers between devices, swap(): return lax.ppermute(value, axis, pairs + [(b, a) for a, b in pairs])  17.3 us
    pallas_call x6, Pallas kernels, call(): pl.pallas_call(body, out_shape=shapes, in_specs=[whole() for _ in args],...  7.1 us
    all_to_all x1, starting transfers between devices, exchange(): lax.all_to_all(value.reshape(count, 1, 128), ('gz', 'ma'), 0, 0, tiled=True)  5.8 us
    unnamed x16, local copies, waits for them, and re-layouts  3.52 us
    all_to_all x1, waiting for transfers between devices, exchange(): lax.all_to_all(value.reshape(count, 1, 128), ('gz', 'ma'), 0, 0, tiled=True)  3.19 us
  transfers between devices with their start and end apart: 7, of which 4 were waited for; matrix products, arithmetic and copies ran while one was open for 0% of the time, Pallas kernels for 1%

profile of v3, /device:TPU:1, one launch (start us, length us, event | category | flops | bytes accessed | tf_op | source)
XLA Modules:
  0.0 96.9 jit_solution(15953874915034424267)
XLA Ops:
  0.6 4.9 %collective-permute-start.2 = (s32[1,128,512]{2,1,0:T(8,128)}, s32[1,128,512]{2,1,0:T(8,128)S(1)}, u32[]{:S(2)}, u32[]{:S(2)}) collective-permute-start(s32[1,128,512]{2,1,0:T(8,128)} %phase.3), channel_id=1, source_target_pairs={{4,8},{12,16},{20,24},{28,32},{36,40},{44,48},{52,56},{60,64},{68,... | collective-permute-start | bytes 786440 | tf_op jit(solution)/shard_map/ppermute | solution.py:324
  5.6 0.0 copy-start
  5.6 1.4 %copy-done = f32[6,1,128,512]{3,2,1,0:T(8,128)S(1)} copy-done((f32[6,1,128,512]{3,2,1,0:T(8,128)S(1)}, f32[6,1,128,512]{3,2,1,0:T(8,128)}, u32[]{:S(2)}) %copy-start) | copy-done | bytes 1572888
  7.0 0.0 copy-start.1
  7.0 1.1 %copy-done.1 = f32[3,1,128,512]{3,2,1,0:T(8,128)S(1)} copy-done((f32[3,1,128,512]{3,2,1,0:T(8,128)S(1)}, f32[3,1,128,512]{3,2,1,0:T(8,128)}, u32[]{:S(2)}) %copy-start.1) | copy-done | bytes 786456
  8.1 0.0 copy-start.2
  8.1 0.9 copy-done.2
  9.1 0.0 copy-start.5
  9.1 0.7 collective-permute-done.2.far_phase.phase
  9.8 0.5 shard_map.97
  10.3 0.1 collective-permute-start.4
  10.4 3.9 %collective-permute-start.3 = (f32[264,512]{1,0:T(8,128)S(1)}, f32[264,512]{1,0:T(8,128)S(1)}, u32[]{:S(2)}, u32[]{:S(2)}) collective-permute-start(f32[264,512]{1,0:T(8,128)S(1)} %get-tuple-element.13), channel_id=1, source_target_pairs={{4,8},{12,16},{20,24},{28,32},{36,40},{44,48},{52,56},{60,64},{68,... | collective-permute-start | bytes 1622024 | tf_op jit(solution)/shard_map/ppermute | solution.py:324
  14.3 0.0 copy-start.3
  14.4 0.0 copy-start.4
  14.4 0.8 collective-permute-start.1
  15.2 3.8 %collective-permute-start = (f32[8,512]{1,0:T(8,128)S(1)}, f32[8,512]{1,0:T(8,128)S(1)}, u32[]{:S(2)}, u32[]{:S(2)}) collective-permute-start(f32[8,512]{1,0:T(8,128)S(1)} %get-tuple-element.10._), channel_id=1, source_target_pairs={{0,1},{2,3},{1,0},{3,2},{4,5},{6,7},{5,4},{7,6},{8,9},{10,11},{9,8... | collective-permute-start | bytes 49160 | tf_op jit(solution)/shard_map/ppermute | solution.py:324
  18.9 0.0 collective-permute-done.1.odd_row
  18.9 1.1 %collective-permute-done.even_row = f32[8,512]{1,0:T(8,128)S(1)} collective-permute-done((f32[8,512]{1,0:T(8,128)S(1)}, f32[8,512]{1,0:T(8,128)S(1)}, u32[]{:S(2)}, u32[]{:S(2)}) %collective-permute-start) | collective-permute-done | bytes 16416 | tf_op jit(solution)/shard_map/ppermute | solution.py:324
  20.1 0.0 copy-done.5
  20.1 1.4 %shard_map.96 = (f32[3,128,512]{2,1,0:T(8,128)S(1)}, f32[2,128,512]{2,1,0:T(8,128)S(1)}) custom-call(f32[3,1,128,512]{3,2,1,0:T(8,128)S(1)} %copy-done.1, f32[6,1,128,512]{3,2,1,0:T(8,128)S(1)} %copy-done, s32[1,128,512]{2,1,0:T(8,128)S(1)} %copy-done.5, f32[1,128,512]{2,1,0:T(8,128)S(1)} %copy-done.2, f32[8,512]{1,0:T(8,128)S(1)} %collective-permute-done.even_row, ...), custom_call_target="tpu_custom_call" | custom-call | flops 8000000 | bytes 4489216 | tf_op jit(solution)/shard_map/pallas_call | solution.py:55
  21.5 0.0 collective-permute-done.3.far
  21.5 0.0 collective-permute-done.4.near
  21.5 0.0 copy-done.3
  21.5 0.0 copy-done.4
  21.5 0.0 copy-start.6
  21.5 0.0 copy-start.7
  21.5 1.2 %shard_map.98 = (f32[3,128,512]{2,1,0:T(8,128)S(1)}, f32[1280,128]{1,0:T(8,128)S(1)}) custom-call(f32[3,128,512]{2,1,0:T(8,128)S(1)} %get-tuple-element.12.local, f32[264,512]{1,0:T(8,128)S(1)} %collective-permute-done.3.far, f32[6,128,512]{2,1,0:T(8,128)S(1)} %collective-permute-done.4.near, s32[1,128,512]{2,1,0:T(8,128)S(1)} %copy-done.5, ...), custom_call_target="tpu_custom_call" | custom-call | flops 600000000 | bytes 5652480 | tf_op jit(solution)/shard_map/pallas_call | solution.py:55
  22.8 40.2 %all_to_all.10 = f32[1280,1,128]{2,1,0:T(1,128)S(1)} all-to-all(f32[1280,1,128]{2,1,0:T(1,128)S(1)} %bitcast.9), channel_id=1, replica_groups=mesh['gz'=64,'ma'=4] {'gz','ma'}, dimensions={0} | all-to-all | bytes 1310720 | tf_op jit(solution)/shard_map/all_to_all | solution.py:357
  63.0 0.0 copy-done.6
  63.0 0.0 copy-done.7
  63.0 2.3 %shard_map.99 = f32[1280,128]{1,0:T(8,128)} custom-call(f32[1280,128]{1,0:T(8,128)S(1)} %bitcast.10, f32[8,128]{1,0:T(8,128)S(1)} %copy-done.7, f32[8,256]{1,0:T(8,128)S(1)} %copy-done.6, bf16[512,512]{1,0:T(8,128)(2,1)S(1)} %copy-done.4, bf16[512,512]{1,0:T(8,128)(2,1)S(1)} %copy-done.3), custom_call_target="tpu_custom_call" | custom-call | flops 700000000 | bytes 2371584 | tf_op jit(solution)/shard_map/pallas_call | solution.py:55
  65.3 5.8 %all-to-all-start.1 = ((f32[1280,1,128]{2,1,0:T(1,128)}), f32[1280,1,128]{2,1,0:T(1,128)S(1)}, u32[]{:S(2)}, u32[]{:S(2)}) async-start(f32[1280,1,128]{2,1,0:T(1,128)} %bitcast.4), calls=%async_computation.1 | async-start | bytes 1310720 | tf_op jit(solution)/shard_map/all_to_all | solution.py:357
  71.1 3.8 %collective-permute-start.5 = (f32[2,128,512]{2,1,0:T(8,128)S(1)}, f32[2,128,512]{2,1,0:T(8,128)S(1)}, u32[]{:S(2)}, u32[]{:S(2)}) collective-permute-start(f32[2,128,512]{2,1,0:T(8,128)S(1)} %get-tuple-element.17), channel_id=1, source_target_pairs={{4,8},{12,16},{20,24},{28,32},{36,40},{44,48},{52,56},{60,64},{68,... | collective-permute-start | bytes 1572872 | tf_op jit(solution)/shard_map/ppermute | solution.py:324
  75.0 17.1 %collective-permute-done.5.later = f32[2,128,512]{2,1,0:T(8,128)S(1)} collective-permute-done((f32[2,128,512]{2,1,0:T(8,128)S(1)}, f32[2,128,512]{2,1,0:T(8,128)S(1)}, u32[]{:S(2)}, u32[]{:S(2)}) %collective-permute-start.5) | collective-permute-done | bytes 524320 | tf_op jit(solution)/shard_map/ppermute | solution.py:324
  92.0 3.2 %all-to-all-done.1 = f32[1280,1,128]{2,1,0:T(1,128)S(1)} async-done(((f32[1280,1,128]{2,1,0:T(1,128)}), f32[1280,1,128]{2,1,0:T(1,128)S(1)}, u32[]{:S(2)}, u32[]{:S(2)}) %all-to-all-start.1) | async-done | bytes 655392 | tf_op jit(solution)/shard_map/all_to_all | solution.py:357
  95.2 1.7 %shard_map.100 = (f32[3,1,128,512]{3,2,1,0:T(8,128)}, f32[1,128,512]{2,1,0:T(8,128)}) custom-call(f32[1280,128]{1,0:T(8,128)S(1)} %bitcast.8, f32[3,128,512]{2,1,0:T(8,128)S(1)} %get-tuple-element.16.u, f32[2,128,512]{2,1,0:T(8,128)S(1)} %collective-permute-done.5.later, bf16[512,512]{1,0:T(8,128)(2,1)S(1)} %copy-done.4, bf16[512,512]{1,0:T(8,128)(2,1)S(1)} %copy-done.3), custom_call_target="tpu_custom_call" | custom-call | flops 500000000 | bytes 4063232 | tf_op jit(solution)/shard_map/pallas_call | solution.py:55
  (1 shorter events, 0.0 us)
Async XLA Ops:
  0.6 9.2 %collective-permute-start.2 = (s32[1,128,512]{2,1,0:T(8,128)}, s32[1,128,512]{2,1,0:T(8,128)S(1)}, u32[]{:S(2)}, u32[]{:S(2)}) collective-permute-start(s32[1,128,512]{2,1,0:T(8,128)} %phase.3), channel_id=1, source_target_pairs={{4,8},{12,16},{20,24},{28,32},{36,40},{44,48},{52,56},{60,64},{68,... | collective-permute-start | bytes 786440 | tf_op jit(solution)/shard_map/ppermute | solution.py:324
  5.6 1.4 %copy-start = (f32[6,1,128,512]{3,2,1,0:T(8,128)S(1)}, f32[6,1,128,512]{3,2,1,0:T(8,128)}, u32[]{:S(2)}) copy-start(f32[6,1,128,512]{3,2,1,0:T(8,128)} %stress.5) | copy-start | bytes 4718596
  7.0 1.1 %copy-start.1 = (f32[3,1,128,512]{3,2,1,0:T(8,128)S(1)}, f32[3,1,128,512]{3,2,1,0:T(8,128)}, u32[]{:S(2)}) copy-start(f32[3,1,128,512]{3,2,1,0:T(8,128)} %pred_.5) | copy-start | bytes 2359300
  8.1 0.9 copy-start.2
  9.1 11.0 %copy-start.5 = (s32[1,128,512]{2,1,0:T(8,128)S(1)}, s32[1,128,512]{2,1,0:T(8,128)}, u32[]{:S(2)}) copy-start(s32[1,128,512]{2,1,0:T(8,128)} %phase.3) | copy-start | bytes 786436
  10.3 11.2 %collective-permute-start.4 = (f32[6,128,512]{2,1,0:T(8,128)S(1)}, f32[6,128,512]{2,1,0:T(8,128)S(1)}, u32[]{:S(2)}, u32[]{:S(2)}) collective-permute-start(f32[6,128,512]{2,1,0:T(8,128)S(1)} %get-tuple-element.14), channel_id=1, source_target_pairs={{0,4},{8,12},{16,20},{24,28},{32,36},{40,44},{48,52},{56,60},{64,6... | collective-permute-start | bytes 4718600 | tf_op jit(solution)/shard_map/ppermute | solution.py:324
  10.4 11.1 %collective-permute-start.3 = (f32[264,512]{1,0:T(8,128)S(1)}, f32[264,512]{1,0:T(8,128)S(1)}, u32[]{:S(2)}, u32[]{:S(2)}) collective-permute-start(f32[264,512]{1,0:T(8,128)S(1)} %get-tuple-element.13), channel_id=1, source_target_pairs={{4,8},{12,16},{20,24},{28,32},{36,40},{44,48},{52,56},{60,64},{68,... | collective-permute-start | bytes 1622024 | tf_op jit(solution)/shard_map/ppermute | solution.py:324
  14.3 7.2 %copy-start.3 = (bf16[512,512]{1,0:T(8,128)(2,1)S(1)}, bf16[512,512]{1,0:T(8,128)(2,1)}, u32[]{:S(2)}) copy-start(bf16[512,512]{1,0:T(8,128)(2,1)} %constant.9.clone.low.refs_4_) | copy-start | bytes 1572868
  14.4 7.2 %copy-start.4 = (bf16[512,512]{1,0:T(8,128)(2,1)S(1)}, bf16[512,512]{1,0:T(8,128)(2,1)}, u32[]{:S(2)}) copy-start(bf16[512,512]{1,0:T(8,128)(2,1)} %constant.8.clone.high.refs_3_) | copy-start | bytes 1572868
  14.4 4.6 %collective-permute-start.1 = (f32[8,512]{1,0:T(8,128)S(1)}, f32[8,512]{1,0:T(8,128)S(1)}, u32[]{:S(2)}, u32[]{:S(2)}) collective-permute-start(f32[8,512]{1,0:T(8,128)S(1)} %get-tuple-element.11), channel_id=1, source_target_pairs={{1,2},{2,1},{5,6},{6,5},{9,10},{10,9},{13,14},{14,13},{17,18},{18,... | collective-permute-start | bytes 49160 | tf_op jit(solution)/shard_map/ppermute | solution.py:324
  15.2 4.9 %collective-permute-start = (f32[8,512]{1,0:T(8,128)S(1)}, f32[8,512]{1,0:T(8,128)S(1)}, u32[]{:S(2)}, u32[]{:S(2)}) collective-permute-start(f32[8,512]{1,0:T(8,128)S(1)} %get-tuple-element.10._), channel_id=1, source_target_pairs={{0,1},{2,3},{1,0},{3,2},{4,5},{6,7},{5,4},{7,6},{8,9},{10,11},{9,8... | collective-permute-start | bytes 49160 | tf_op jit(solution)/shard_map/ppermute | solution.py:324
  21.5 41.5 %copy-start.6 = (f32[8,256]{1,0:T(8,128)S(1)}, f32[8,256]{1,0:T(8,128)}, u32[]{:S(2)}) copy-start(f32[8,256]{1,0:T(8,128)} %constant.11.clone.refs_2_) | copy-start | bytes 24580
  21.5 41.5 %copy-start.7 = (f32[8,128]{1,0:T(8,128)S(1)}, f32[8,128]{1,0:T(8,128)}, u32[]{:S(2)}) copy-start(f32[8,128]{1,0:T(8,128)} %constant.10.clone.refs_1_) | copy-start | bytes 12292
  65.3 29.9 %all-to-all-start.1 = ((f32[1280,1,128]{2,1,0:T(1,128)}), f32[1280,1,128]{2,1,0:T(1,128)S(1)}, u32[]{:S(2)}, u32[]{:S(2)}) async-start(f32[1280,1,128]{2,1,0:T(1,128)} %bitcast.4), calls=%async_computation.1 | async-start | bytes 1310720 | tf_op jit(solution)/shard_map/all_to_all | solution.py:357
  71.1 20.9 %collective-permute-start.5 = (f32[2,128,512]{2,1,0:T(8,128)S(1)}, f32[2,128,512]{2,1,0:T(8,128)S(1)}, u32[]{:S(2)}, u32[]{:S(2)}) collective-permute-start(f32[2,128,512]{2,1,0:T(8,128)S(1)} %get-tuple-element.17), channel_id=1, source_target_pairs={{4,8},{12,16},{20,24},{28,32},{36,40},{44,48},{52,56},{60,64},{68,... | collective-permute-start | bytes 1572872 | tf_op jit(solution)/shard_map/ppermute | solution.py:324

commit v4 on v2

--- a/solution.py
+++ b/solution.py
@@ -264,7 +264,13 @@
         sent[pl.ds(5 * b + 4, planes, step)] = edge
 
 
-def final_body(received, u, later, high, low, velocity, pressure, made, arrived):
+def whole_body(u, later, out):
+    out[0] = u[0] + later[0]
+    out[1] = u[1] + later[1]
+    out[2] = u[2]
+
+
+def final_body(received, u, high, low, velocity, pressure, made, arrived):
     pairs = received.shape[0] // 5
     table = (high[...], low[...])
     nn = ((1,), (0,))
@@ -281,13 +287,13 @@
     made[3] = p
     copies[3].start()
     left, right = shifted_y(p)
-    made[1] = u[1] + later[1] - 0.25 * (right - left)
+    made[1] = u[1] - 0.25 * (right - left)
     copies[1].start()
     ends = split(received[pl.ds(4, pairs, 5)].T[0:8])
     lead = product_3(ends, (high[:pairs], low[:pairs]), nn)
     trail = product_3(ends, (high[pairs:], low[pairs:]), nn)
     behind, ahead = shifted(p, lead[0:1] + trail[2:3], lead[1:2] + trail[3:4])
-    made[0] = u[0] + later[0] - 0.25 * (ahead - behind)
+    made[0] = u[0] - 0.25 * (ahead - behind)
     copies[0].start()
     for copy in copies:
         copy.wait()
@@ -346,16 +352,17 @@
         lambda *refs: solve_body(lines, *refs),
         [(5 * devices, 128)],
         (exchange(modes), part_x, part_y, high, low),
-        700000000,
+        20000000000,
         (
             pltpu.VMEM((2 * tiles * planes_z, 128), F32),
             pltpu.VMEM((2 * tiles * (planes_z + 2), 128), F32),
         ),
     )
+    (u,) = call(whole_body, [(3, rows, columns)], (u, later), 20000000000)
     velocity, pressure = call(
         final_body,
         [(3, 1, rows, columns), (1, rows, columns)],
-        (exchange(solved), u, later, high, low),
+        (exchange(solved), u, high, low),
         500000000,
         (pltpu.VMEM((4, rows, columns), F32), pltpu.SemaphoreType.DMA((4,))),
         pl.ANY,

time: 97.4 us -> 98.9 us (1.015)
  blocking collectives: 40.2 us -> 0 us
  waiting for transfers between devices: 22.1 us -> 45.2 us
  starting transfers between devices: 23.1 us -> 39.7 us
  Pallas kernels: 7.23 us -> 9.19 us
    all_to_all x1 -> x0, blocking collectives: 40.2 us -> none  [exchange(): lax.all_to_all(value.reshape(count, 1, 128), ('gz', 'ma'), 0, 0, tiled=True)]
    all_to_all x1 -> x2, waiting for transfers between devices: 3.19 us -> 43.3 us  [exchange(): lax.all_to_all(value.reshape(count, 1, 128), ('gz', 'ma'), 0, 0, tiled=True)]
    ppermute x6, waiting for transfers between devices: 18.9 us -> 1.87 us  [swap(): return lax.ppermute(value, axis, pairs + [(b, a) for a, b in pairs])]
    all_to_all x1 -> x2, starting transfers between devices: 5.8 us -> 22.6 us  [exchange(): lax.all_to_all(value.reshape(count, 1, 128), ('gz', 'ma'), 0, 0, tiled=True)]
    pallas_call x6 -> x7, Pallas kernels: 7.23 us -> 9.19 us  [call(): pl.pallas_call(body, out_shape=shapes, in_specs=[whole() for _ in args],...]
  transfers between devices with their start and end apart: 7 -> 8, of which waited for: 4 -> 4; matrix products, arithmetic and copies ran while one was open for 0% -> 0% of each run, Pallas kernels for 1% -> 5%
where the time goes in v4:
time: 98.9 us; the launch traced here: 98.4 us
  waiting for transfers between devices  45.2 us (46%)
  starting transfers between devices  39.7 us (40%)
  Pallas kernels  9.19 us (9%)
  local copies, waits for them, and re-layouts  3.52 us (4%)
    all_to_all x2, waiting for transfers between devices, exchange(): lax.all_to_all(value.reshape(count, 1, 128), ('gz', 'ma'), 0, 0, tiled=True)  43.3 us
    all_to_all x2, starting transfers between devices, exchange(): lax.all_to_all(value.reshape(count, 1, 128), ('gz', 'ma'), 0, 0, tiled=True)  22.6 us
    ppermute x6, starting transfers between devices, swap(): return lax.ppermute(value, axis, pairs + [(b, a) for a, b in pairs])  17.2 us
    pallas_call x7, Pallas kernels, call(): pl.pallas_call(body, out_shape=shapes, in_specs=[whole() for _ in args],...  9.19 us
    unnamed x16, local copies, waits for them, and re-layouts  3.52 us
  transfers between devices with their start and end apart: 8, of which 4 were waited for; matrix products, arithmetic and copies ran while one was open for 0% of the time, Pallas kernels for 5%

profile of v4, /device:TPU:1, one launch (start us, length us, event | category | flops | bytes accessed | tf_op | source)
XLA Modules:
  0.0 98.4 jit_solution(13993105465809203038)
XLA Ops:
  0.6 4.9 %collective-permute-start.2 = (s32[1,128,512]{2,1,0:T(8,128)}, s32[1,128,512]{2,1,0:T(8,128)S(1)}, u32[]{:S(2)}, u32[]{:S(2)}) collective-permute-start(s32[1,128,512]{2,1,0:T(8,128)} %phase.3), channel_id=1, source_target_pairs={{4,8},{12,16},{20,24},{28,32},{36,40},{44,48},{52,56},{60,64},{68,... | collective-permute-start | bytes 786440 | tf_op jit(solution)/shard_map/ppermute | solution.py:312
  5.6 0.0 copy-start
  5.6 1.4 %copy-done = f32[6,1,128,512]{3,2,1,0:T(8,128)S(1)} copy-done((f32[6,1,128,512]{3,2,1,0:T(8,128)S(1)}, f32[6,1,128,512]{3,2,1,0:T(8,128)}, u32[]{:S(2)}) %copy-start) | copy-done | bytes 1572888
  7.0 0.0 copy-start.1
  7.0 1.1 %copy-done.1 = f32[3,1,128,512]{3,2,1,0:T(8,128)S(1)} copy-done((f32[3,1,128,512]{3,2,1,0:T(8,128)S(1)}, f32[3,1,128,512]{3,2,1,0:T(8,128)}, u32[]{:S(2)}) %copy-start.1) | copy-done | bytes 786456
  8.1 0.0 copy-start.2
  8.1 0.9 copy-done.2
  9.1 0.0 copy-start.5
  9.1 0.7 collective-permute-done.2.far_phase.phase
  9.8 0.5 shard_map.97
  10.3 0.1 collective-permute-start.4
  10.4 3.9 %collective-permute-start.3 = (f32[264,512]{1,0:T(8,128)S(1)}, f32[264,512]{1,0:T(8,128)S(1)}, u32[]{:S(2)}, u32[]{:S(2)}) collective-permute-start(f32[264,512]{1,0:T(8,128)S(1)} %get-tuple-element.13), channel_id=1, source_target_pairs={{4,8},{12,16},{20,24},{28,32},{36,40},{44,48},{52,56},{60,64},{68,... | collective-permute-start | bytes 1622024 | tf_op jit(solution)/shard_map/ppermute | solution.py:312
  14.3 0.0 copy-start.3
  14.4 0.0 copy-start.4
  14.4 0.8 collective-permute-start.1
  15.2 3.8 %collective-permute-start = (f32[8,512]{1,0:T(8,128)S(1)}, f32[8,512]{1,0:T(8,128)S(1)}, u32[]{:S(2)}, u32[]{:S(2)}) collective-permute-start(f32[8,512]{1,0:T(8,128)S(1)} %get-tuple-element.10._), channel_id=1, source_target_pairs={{0,1},{2,3},{1,0},{3,2},{4,5},{6,7},{5,4},{7,6},{8,9},{10,11},{9,8... | collective-permute-start | bytes 49160 | tf_op jit(solution)/shard_map/ppermute | solution.py:312
  18.9 0.0 collective-permute-done.1.odd_row
  18.9 1.1 %collective-permute-done.even_row = f32[8,512]{1,0:T(8,128)S(1)} collective-permute-done((f32[8,512]{1,0:T(8,128)S(1)}, f32[8,512]{1,0:T(8,128)S(1)}, u32[]{:S(2)}, u32[]{:S(2)}) %collective-permute-start) | collective-permute-done | bytes 16416 | tf_op jit(solution)/shard_map/ppermute | solution.py:312
  20.1 0.0 copy-done.5
  20.1 1.4 %shard_map.96 = (f32[3,128,512]{2,1,0:T(8,128)S(1)}, f32[2,128,512]{2,1,0:T(8,128)S(1)}) custom-call(f32[3,1,128,512]{3,2,1,0:T(8,128)S(1)} %copy-done.1, f32[6,1,128,512]{3,2,1,0:T(8,128)S(1)} %copy-done, s32[1,128,512]{2,1,0:T(8,128)S(1)} %copy-done.5, f32[1,128,512]{2,1,0:T(8,128)S(1)} %copy-done.2, f32[8,512]{1,0:T(8,128)S(1)} %collective-permute-done.even_row, ...), custom_call_target="tpu_custom_call" | custom-call | flops 8000000 | bytes 4489216 | tf_op jit(solution)/shard_map/pallas_call | solution.py:55
  21.5 0.0 collective-permute-done.3.far
  21.5 0.0 collective-permute-done.4.near
  21.5 0.0 copy-done.3
  21.5 0.0 copy-done.4
  21.5 0.0 copy-start.6
  21.5 0.0 copy-start.7
  21.5 2.1 %shard_map.98 = (f32[3,128,512]{2,1,0:T(8,128)S(1)}, f32[1280,128]{1,0:T(8,128)}) custom-call(f32[3,128,512]{2,1,0:T(8,128)S(1)} %get-tuple-element.12.local, f32[264,512]{1,0:T(8,128)S(1)} %collective-permute-done.3.far, f32[6,128,512]{2,1,0:T(8,128)S(1)} %collective-permute-done.4.near, s32[1,128,512]{2,1,0:T(8,128)S(1)} %copy-done.5, ...), custom_call_target="tpu_custom_call" | custom-call | flops 600000000 | bytes 5652480 | tf_op jit(solution)/shard_map/pallas_call | solution.py:55
  23.6 16.4 %all-to-all-start = ((f32[1280,1,128]{2,1,0:T(1,128)}), f32[1280,1,128]{2,1,0:T(1,128)S(1)}, u32[]{:S(2)}, u32[]{:S(2)}) async-start(f32[1280,1,128]{2,1,0:T(1,128)} %bitcast.1), calls=%async_computation | async-start | bytes 1310720 | tf_op jit(solution)/shard_map/all_to_all | solution.py:345
  40.0 3.7 %collective-permute-start.5 = (f32[2,128,512]{2,1,0:T(8,128)S(1)}, f32[2,128,512]{2,1,0:T(8,128)}, u32[]{:S(2)}, u32[]{:S(2)}) collective-permute-start(f32[2,128,512]{2,1,0:T(8,128)S(1)} %get-tuple-element.17), channel_id=1, source_target_pairs={{4,8},{12,16},{20,24},{28,32},{36,40},{44,48},{52,56},{60,64},{68,... | collective-permute-start | bytes 1572872 | tf_op jit(solution)/shard_map/ppermute | solution.py:312
  43.7 20.3 %all-to-all-done = f32[1280,1,128]{2,1,0:T(1,128)S(1)} async-done(((f32[1280,1,128]{2,1,0:T(1,128)}), f32[1280,1,128]{2,1,0:T(1,128)S(1)}, u32[]{:S(2)}, u32[]{:S(2)}) %all-to-all-start) | async-done | bytes 655392 | tf_op jit(solution)/shard_map/all_to_all | solution.py:345
  63.9 0.0 copy-done.6
  63.9 0.0 copy-done.7
  63.9 2.4 %shard_map.99 = f32[1280,128]{1,0:T(8,128)} custom-call(f32[1280,128]{1,0:T(8,128)S(1)} %bitcast.9, f32[8,128]{1,0:T(8,128)S(1)} %copy-done.7, f32[8,256]{1,0:T(8,128)S(1)} %copy-done.6, bf16[512,512]{1,0:T(8,128)(2,1)S(1)} %copy-done.4, bf16[512,512]{1,0:T(8,128)(2,1)S(1)} %copy-done.3), custom_call_target="tpu_custom_call" | custom-call | flops 20000000000 | bytes 2371584 | tf_op jit(solution)/shard_map/pallas_call | solution.py:55
  66.4 6.2 %all-to-all-start.1 = ((f32[1280,1,128]{2,1,0:T(1,128)}), f32[1280,1,128]{2,1,0:T(1,128)S(1)}, u32[]{:S(2)}, u32[]{:S(2)}) async-start(f32[1280,1,128]{2,1,0:T(1,128)} %bitcast.4), calls=%async_computation.1 | async-start | bytes 1310720 | tf_op jit(solution)/shard_map/all_to_all | solution.py:345
  72.6 0.0 collective-permute-done.5.later
  72.6 1.1 %shard_map.100.u = f32[3,128,512]{2,1,0:T(8,128)S(1)} custom-call(f32[3,128,512]{2,1,0:T(8,128)S(1)} %get-tuple-element.16.u, f32[2,128,512]{2,1,0:T(8,128)} %collective-permute-done.5.later), custom_call_target="tpu_custom_call" | custom-call | flops 20000000000 | bytes 2097152 | tf_op jit(solution)/shard_map/pallas_call | solution.py:55
  73.7 23.1 %all-to-all-done.1 = f32[1280,1,128]{2,1,0:T(1,128)S(1)} async-done(((f32[1280,1,128]{2,1,0:T(1,128)}), f32[1280,1,128]{2,1,0:T(1,128)S(1)}, u32[]{:S(2)}, u32[]{:S(2)}) %all-to-all-start.1) | async-done | bytes 655392 | tf_op jit(solution)/shard_map/all_to_all | solution.py:345
  96.8 1.7 %shard_map.101 = (f32[3,1,128,512]{3,2,1,0:T(8,128)}, f32[1,128,512]{2,1,0:T(8,128)}) custom-call(f32[1280,128]{1,0:T(8,128)S(1)} %bitcast.8, f32[3,128,512]{2,1,0:T(8,128)S(1)} %shard_map.100.u, bf16[512,512]{1,0:T(8,128)(2,1)S(1)} %copy-done.4, bf16[512,512]{1,0:T(8,128)(2,1)S(1)} %copy-done.3), custom_call_target="tpu_custom_call" | custom-call | flops 500000000 | bytes 3538944 | tf_op jit(solution)/shard_map/pallas_call | solution.py:55
  (1 shorter events, 0.0 us)
Async XLA Ops:
  0.6 9.2 %collective-permute-start.2 = (s32[1,128,512]{2,1,0:T(8,128)}, s32[1,128,512]{2,1,0:T(8,128)S(1)}, u32[]{:S(2)}, u32[]{:S(2)}) collective-permute-start(s32[1,128,512]{2,1,0:T(8,128)} %phase.3), channel_id=1, source_target_pairs={{4,8},{12,16},{20,24},{28,32},{36,40},{44,48},{52,56},{60,64},{68,... | collective-permute-start | bytes 786440 | tf_op jit(solution)/shard_map/ppermute | solution.py:312
  5.6 1.4 %copy-start = (f32[6,1,128,512]{3,2,1,0:T(8,128)S(1)}, f32[6,1,128,512]{3,2,1,0:T(8,128)}, u32[]{:S(2)}) copy-start(f32[6,1,128,512]{3,2,1,0:T(8,128)} %stress.5) | copy-start | bytes 4718596
  7.0 1.1 %copy-start.1 = (f32[3,1,128,512]{3,2,1,0:T(8,128)S(1)}, f32[3,1,128,512]{3,2,1,0:T(8,128)}, u32[]{:S(2)}) copy-start(f32[3,1,128,512]{3,2,1,0:T(8,128)} %pred_.5) | copy-start | bytes 2359300
  8.1 0.9 copy-start.2
  9.1 11.0 %copy-start.5 = (s32[1,128,512]{2,1,0:T(8,128)S(1)}, s32[1,128,512]{2,1,0:T(8,128)}, u32[]{:S(2)}) copy-start(s32[1,128,512]{2,1,0:T(8,128)} %phase.3) | copy-start | bytes 786436
  10.3 11.2 %collective-permute-start.4 = (f32[6,128,512]{2,1,0:T(8,128)S(1)}, f32[6,128,512]{2,1,0:T(8,128)S(1)}, u32[]{:S(2)}, u32[]{:S(2)}) collective-permute-start(f32[6,128,512]{2,1,0:T(8,128)S(1)} %get-tuple-element.14), channel_id=1, source_target_pairs={{0,4},{8,12},{16,20},{24,28},{32,36},{40,44},{48,52},{56,60},{64,6... | collective-permute-start | bytes 4718600 | tf_op jit(solution)/shard_map/ppermute | solution.py:312
  10.4 11.1 %collective-permute-start.3 = (f32[264,512]{1,0:T(8,128)S(1)}, f32[264,512]{1,0:T(8,128)S(1)}, u32[]{:S(2)}, u32[]{:S(2)}) collective-permute-start(f32[264,512]{1,0:T(8,128)S(1)} %get-tuple-element.13), channel_id=1, source_target_pairs={{4,8},{12,16},{20,24},{28,32},{36,40},{44,48},{52,56},{60,64},{68,... | collective-permute-start | bytes 1622024 | tf_op jit(solution)/shard_map/ppermute | solution.py:312
  14.3 7.2 %copy-start.3 = (bf16[512,512]{1,0:T(8,128)(2,1)S(1)}, bf16[512,512]{1,0:T(8,128)(2,1)}, u32[]{:S(2)}) copy-start(bf16[512,512]{1,0:T(8,128)(2,1)} %constant.9.clone.low.refs_4_) | copy-start | bytes 1572868
  14.4 7.2 %copy-start.4 = (bf16[512,512]{1,0:T(8,128)(2,1)S(1)}, bf16[512,512]{1,0:T(8,128)(2,1)}, u32[]{:S(2)}) copy-start(bf16[512,512]{1,0:T(8,128)(2,1)} %constant.8.clone.high.refs_3_) | copy-start | bytes 1572868
  14.4 4.6 %collective-permute-start.1 = (f32[8,512]{1,0:T(8,128)S(1)}, f32[8,512]{1,0:T(8,128)S(1)}, u32[]{:S(2)}, u32[]{:S(2)}) collective-permute-start(f32[8,512]{1,0:T(8,128)S(1)} %get-tuple-element.11), channel_id=1, source_target_pairs={{1,2},{2,1},{5,6},{6,5},{9,10},{10,9},{13,14},{14,13},{17,18},{18,... | collective-permute-start | bytes 49160 | tf_op jit(solution)/shard_map/ppermute | solution.py:312
  15.2 4.9 %collective-permute-start = (f32[8,512]{1,0:T(8,128)S(1)}, f32[8,512]{1,0:T(8,128)S(1)}, u32[]{:S(2)}, u32[]{:S(2)}) collective-permute-start(f32[8,512]{1,0:T(8,128)S(1)} %get-tuple-element.10._), channel_id=1, source_target_pairs={{0,1},{2,3},{1,0},{3,2},{4,5},{6,7},{5,4},{7,6},{8,9},{10,11},{9,8... | collective-permute-start | bytes 49160 | tf_op jit(solution)/shard_map/ppermute | solution.py:312
  21.5 42.4 %copy-start.6 = (f32[8,256]{1,0:T(8,128)S(1)}, f32[8,256]{1,0:T(8,128)}, u32[]{:S(2)}) copy-start(f32[8,256]{1,0:T(8,128)} %constant.11.clone.refs_2_) | copy-start | bytes 24580
  21.5 42.4 %copy-start.7 = (f32[8,128]{1,0:T(8,128)S(1)}, f32[8,128]{1,0:T(8,128)}, u32[]{:S(2)}) copy-start(f32[8,128]{1,0:T(8,128)} %constant.10.clone.refs_1_) | copy-start | bytes 12292
  23.6 40.3 %all-to-all-start = ((f32[1280,1,128]{2,1,0:T(1,128)}), f32[1280,1,128]{2,1,0:T(1,128)S(1)}, u32[]{:S(2)}, u32[]{:S(2)}) async-start(f32[1280,1,128]{2,1,0:T(1,128)} %bitcast.1), calls=%async_computation | async-start | bytes 1310720 | tf_op jit(solution)/shard_map/all_to_all | solution.py:345
  40.0 32.6 %collective-permute-start.5 = (f32[2,128,512]{2,1,0:T(8,128)S(1)}, f32[2,128,512]{2,1,0:T(8,128)}, u32[]{:S(2)}, u32[]{:S(2)}) collective-permute-start(f32[2,128,512]{2,1,0:T(8,128)S(1)} %get-tuple-element.17), channel_id=1, source_target_pairs={{4,8},{12,16},{20,24},{28,32},{36,40},{44,48},{52,56},{60,64},{68,... | collective-permute-start | bytes 1572872 | tf_op jit(solution)/shard_map/ppermute | solution.py:312
  66.4 30.4 %all-to-all-start.1 = ((f32[1280,1,128]{2,1,0:T(1,128)}), f32[1280,1,128]{2,1,0:T(1,128)S(1)}, u32[]{:S(2)}, u32[]{:S(2)}) async-start(f32[1280,1,128]{2,1,0:T(1,128)} %bitcast.4), calls=%async_computation.1 | async-start | bytes 1310720 | tf_op jit(solution)/shard_map/all_to_all | solution.py:345
